TPU v7x, 128 devices: a whole 4x4x4 slice. The times are simulated.
128 devices in a mesh: dp: 32 (over y, x, core), vis: 4 (over z).
Axes of the slice: x: 4, y: 4, z: 4, core: 2. Of those that a mesh axis runs over, the one named last changes fastest.
Arguments:
- patches: bfloat16 [65536, 1280], P(('dp', 'vis')), may hold values from -100 to 100
- window_index: int32 [128, 512], P(('dp', 'vis')), may hold values from 0 to 511, each once within a row
- window_live: int32 [128, 8], P(('dp', 'vis')), may hold values from 0 to 64, as said below
- d_merged: bfloat16 [16384, 5120], P(('dp', 'vis')), may hold values from -1 to 1
- w_qkv: bfloat16 [1280, 2880], replicated, may hold values from -20 to 20
- w_out: bfloat16 [960, 1280], replicated, may hold values from -0.1875 to 0.1875
- merge_gain: float32 [1280], replicated, may hold values from 0.1 to 1.9
Outputs:
- merged: bfloat16 [16384, 5120], P(('dp', 'vis'))
- grad_qkv: float32 [1280, 2880], P(('dp', 'vis'))
- grad_out: float32 [960, 1280], P(None, ('dp', 'vis'))
- grad_gain: float32 [1280], P(('dp', 'vis'))
Inputs may be any that keep to these rules, and one draw needn't show every extreme that they name: `window_live`: entry [i, w] gives the live rows of window slot w of device i = dp * 4 + vis: 0 for an empty slot, else a multiple of 4. On every device the slots with live rows come first. In every vis column the 32 owners hold together exactly 128 windows with live rows.
All inputs are finite; a program needn't handle non-finite values.
Results may differ from a plain program's by a relative error of at most 0.018.
Values may be sent and summed in bfloat16 or wider, within the bound.
A program may use at most 192 MiB of HBM per device.

v0:
```python
import jax
import jax.numpy as jnp
from jax import lax
from jax.sharding import PartitionSpec as P

HEADS = 12


EPSILON = 1e-06
NEGATIVE = -1e30


def contract(formula, first_op, second_op):
    return jnp.einsum(formula, first_op, second_op, preferred_element_type=jnp.float32)


def forward(window_rows, live_rows, w_qkv, w_out, merge_gain):
    window_count, win_rows, model_width = window_rows.shape
    inner_width = w_out.shape[0]
    head_width = inner_width // HEADS
    widened = window_rows.astype(jnp.float32)
    normed = (widened * lax.rsqrt(jnp.mean(widened * widened, -1, keepdims=True) + EPSILON)).astype(
        jnp.bfloat16
    )
    packed = contract("bwd,de->bwe", normed, w_qkv).astype(jnp.bfloat16)
    packed = packed.reshape(window_count, win_rows, 3, HEADS, head_width)
    query = packed[:, :, 0]
    key_rows = packed[:, :, 1]
    values = packed[:, :, 2]
    scores = contract("bqhc,bkhc->bhqk", query, key_rows) * head_width ** (-0.5)
    alive = jnp.arange(win_rows)[None, :] < live_rows[:, None]
    scores = jnp.where(alive[:, None, None, :], scores, NEGATIVE)
    probs = jax.nn.softmax(scores, axis=-1)
    probs_low = probs.astype(jnp.bfloat16)
    context = (
        contract("bhqk,bkhc->bqhc", probs_low, values)
        .astype(jnp.bfloat16)
        .reshape(window_count, win_rows, inner_width)
    )
    attended = widened + contract("bwi,id->bwd", context, w_out)
    inverse = lax.rsqrt(jnp.mean(attended * attended, -1, keepdims=True) + EPSILON)
    normalized = attended * inverse
    row_mask = alive[:, :, None].astype(jnp.float32)
    merged = (
        (normalized * merge_gain * row_mask)
        .astype(jnp.bfloat16)
        .reshape(window_count, win_rows // 4, 4 * model_width)
    )
    saved = (
        normed,
        query,
        key_rows,
        values,
        probs,
        probs_low,
        context,
        normalized,
        inverse,
        row_mask,
    )
    return (merged, saved)


def backward(saved, cotangent, w_out, merge_gain):
    normed, query, key_rows, values, probs, probs_low, context, normalized, inverse, row_mask = (
        saved
    )
    window_count, win_rows, model_width = normalized.shape
    head_width = query.shape[-1]
    grad_rows = (
        cotangent.astype(jnp.float32).reshape(window_count, win_rows, model_width) * row_mask
    )
    grad_gain = jnp.sum(grad_rows * normalized, axis=(0, 1))
    scaled = grad_rows * merge_gain
    d_attended = (
        inverse * (scaled - normalized * jnp.mean(scaled * normalized, -1, keepdims=True))
    ).astype(jnp.bfloat16)
    grad_out = contract("bwi,bwd->id", context, d_attended)
    d_context = (
        contract("bwd,id->bwi", d_attended, w_out)
        .astype(jnp.bfloat16)
        .reshape(window_count, win_rows, HEADS, head_width)
    )
    d_values = contract("bhqk,bqhc->bkhc", probs_low, d_context)
    d_probs = contract("bqhc,bkhc->bhqk", d_context, values)
    d_scores = (
        probs * (d_probs - jnp.sum(d_probs * probs, -1, keepdims=True)) * head_width ** (-0.5)
    ).astype(jnp.bfloat16)
    d_query = contract("bhqk,bkhc->bqhc", d_scores, key_rows)
    d_keys = contract("bhqk,bqhc->bkhc", d_scores, query)
    d_packed = (
        jnp.stack([d_query, d_keys, d_values], axis=2)
        .astype(jnp.bfloat16)
        .reshape(window_count, win_rows, -1)
    )
    grad_qkv = contract("bwd,bwe->de", normed, d_packed)
    return (grad_qkv, grad_out, grad_gain)


def on_device(patches, window_index, window_live, d_merged, w_qkv, w_out, merge_gain):
    model_width = patches.shape[1]
    slot_count = window_live.shape[1]
    win_rows = patches.shape[0] // slot_count
    window_rows = jnp.take(patches, window_index[0], axis=0).reshape(
        slot_count, win_rows, model_width
    )
    own_live = window_live[0]
    own_cot = d_merged.reshape(slot_count, win_rows // 4, 4 * model_width)
    ranks = lax.axis_size("dp")
    per_pair = max(1, slot_count // ranks)
    buffer_slots = ranks * per_pair
    capacity = slot_count // 2
    column_live = lax.all_gather(window_live, "dp", axis=0, tiled=True)
    counts = jnp.sum((column_live > 0).astype(jnp.int32), axis=1)
    starts = jnp.cumsum(counts) - counts
    my_rank = lax.axis_index("dp")
    slot_ids = jnp.arange(slot_count, dtype=jnp.int32)
    target = (starts[my_rank] + slot_ids) % ranks * per_pair + slot_ids // ranks
    buffer_ids = jnp.arange(buffer_slots, dtype=jnp.int32)
    route = ((target[None, :] == buffer_ids[:, None]) & (own_live > 0)[None, :]).astype(
        jnp.bfloat16
    )
    senders = buffer_ids // per_pair
    layers = buffer_ids % per_pair
    offsets = (my_rank - starts[senders]) % ranks + layers * ranks
    arrived = jnp.where(
        offsets < counts[senders], column_live[senders, jnp.minimum(offsets, slot_count - 1)], 0
    )
    flags = (arrived > 0).astype(jnp.int32)
    places = jnp.cumsum(flags) - flags
    chosen = (places[None, :] == jnp.arange(capacity, dtype=jnp.int32)[:, None]) & (flags > 0)[
        None, :
    ]
    picker = chosen.astype(jnp.bfloat16)
    vision_live = jnp.sum(jnp.where(chosen, arrived[None, :], 0), axis=1)
    out_rows = contract("sk,kf->sf", route, window_rows.reshape(slot_count, -1)).astype(
        jnp.bfloat16
    )
    out_cot = contract("sk,kf->sf", route, own_cot.reshape(slot_count, -1)).astype(jnp.bfloat16)
    in_rows = lax.all_to_all(out_rows, "dp", split_axis=0, concat_axis=0, tiled=True)
    vision_rows = (
        contract("cs,sf->cf", picker, in_rows)
        .astype(jnp.bfloat16)
        .reshape(capacity, win_rows, model_width)
    )
    vision_merged, saved = forward(vision_rows, vision_live, w_qkv, w_out, merge_gain)
    sent_back = contract("cs,cf->sf", picker, vision_merged.reshape(capacity, -1)).astype(
        jnp.bfloat16
    )
    returned = lax.all_to_all(sent_back, "dp", split_axis=0, concat_axis=0, tiled=True)
    merged = contract("sk,sf->kf", route, returned).astype(jnp.bfloat16)
    in_cot = lax.all_to_all(out_cot, "dp", split_axis=0, concat_axis=0, tiled=True)
    vision_cot = (
        contract("cs,sf->cf", picker, in_cot)
        .astype(jnp.bfloat16)
        .reshape(capacity, win_rows // 4, 4 * model_width)
    )
    grad_qkv, grad_out, grad_gain = backward(saved, vision_cot, w_out, merge_gain)
    total_qkv, total_out, total_gain = (
        lax.psum_scatter(grad_qkv, ("dp", "vis"), scatter_dimension=0, tiled=True),
        lax.psum_scatter(grad_out, ("dp", "vis"), scatter_dimension=1, tiled=True),
        lax.psum_scatter(grad_gain, ("dp", "vis"), scatter_dimension=0, tiled=True),
    )
    merged_rows = merged.reshape(slot_count * (win_rows // 4), 4 * model_width)
    return (merged_rows, total_qkv, total_out, total_gain)


def solution(mesh):
    in_specs = (
        P(("dp", "vis"), None),
        P(("dp", "vis"), None),
        P(("dp", "vis"), None),
        P(("dp", "vis"), None),
        P(),
        P(),
        P(),
    )
    out_specs = (
        P(("dp", "vis"), None),
        P(("dp", "vis"), None),
        P(None, ("dp", "vis")),
        P(("dp", "vis")),
    )
    return jax.shard_map(
        on_device, mesh=mesh, in_specs=in_specs, out_specs=out_specs, check_vma=False
    )
```

profile of v0, /device:TPU:0, one launch (start us, length us, event | category | flops | bytes accessed | tf_op | source)
XLA Modules:
  0.0 565.2 jit_solution(16005841814282089333)
XLA Ops:
  8.0 21.8 %all-gather = s32[32,1,8]{2,1,0:T(1,128)S(1)} all-gather(s32[1,1,8]{2,1,0:T(1,128)} %bitcast.141), channel_id=1, replica_groups=mesh['dp'=32,'vis'=4] {'dp'}, dimensions={0}, use_global_device_ids=true | all-gather | bytes 1056 | tf_op jit(solution)/shard_map/all_gather | solution.py:113
  32.2 5.4 gather_fusion.3
  42.2 5.1 fusion.2
  47.8 8.0 %reduce.6 = bf16[32,81920]{1,0:T(8,128)(2,1)} reduce(bf16[32,1,81920]{2,0,1:T(8,128)(2,1)} %fusion.2, bf16[]{:T(256)} %broadcast.589), dimensions={1}, to_apply=%copy.67.reduce_sub_computation | reduce | bytes 10485762 | tf_op jit(solution)/shard_map/all_to_all | solution.py:140
  55.9 7.6 %reshape.407 = bf16[32,2,40960]{2,1,0:T(2,128)(2,1)} reshape(bf16[32,81920]{1,0:T(8,128)(2,1)} %reduce.6) | data formatting | bytes 10485760
  63.5 5.8 %all-to-all-start = ((bf16[32,2,40960]{2,1,0:T(2,128)(2,1)}), bf16[32,2,40960]{2,1,0:T(2,128)(2,1)}, u32[]{:S(2)}, u32[]{:S(2)}) async-start(bf16[32,2,40960]{2,1,0:T(2,128)(2,1)} %reshape.407), calls=%async_computation | async-start | bytes 10485760 | tf_op jit(solution)/shard_map/all_to_all | solution.py:140
  72.2 5.2 fusion.4
  77.4 8.0 %reduce.7 = bf16[32,81920]{1,0:T(8,128)(2,1)} reduce(bf16[32,1,81920]{2,0,1:T(8,128)(2,1)} %fusion.4, bf16[]{:T(256)} %broadcast.589), dimensions={1}, to_apply=%copy.74.reduce_sub_computation | reduce | bytes 10485762 | tf_op jit(solution)/shard_map/all_to_all | solution.py:152
  85.4 7.6 %reshape.411 = bf16[32,2,40960]{2,1,0:T(2,128)(2,1)} reshape(bf16[32,81920]{1,0:T(8,128)(2,1)} %reduce.7) | data formatting | bytes 10485760
  93.0 42.0 %all-to-all-done = bf16[32,2,40960]{2,1,0:T(2,128)(2,1)} async-done(((bf16[32,2,40960]{2,1,0:T(2,128)(2,1)}), bf16[32,2,40960]{2,1,0:T(2,128)(2,1)}, u32[]{:S(2)}, u32[]{:S(2)}) %all-to-all-start) | async-done | bytes 5242912 | tf_op jit(solution)/shard_map/all_to_all | solution.py:140
  135.0 4.9 all-to-all-start.2
  142.6 21.0 %reshape.408 = bf16[32,1,81920]{2,1,0:T(2,128)(2,1)} reshape(bf16[32,2,40960]{2,1,0:T(2,128)(2,1)} %all-to-all-done) | data formatting | bytes 10485760
  163.6 9.7 %fusion.5 = f32[4,81920]{1,0:T(4,128)S(1)} fusion(pred[4,32]{1,0:T(4,128)(4,1)S(1)} %get-tuple-element.9, bf16[32,1,81920]{2,1,0:T(2,128)(2,1)} %reshape.408), kind=kOutput, calls=%fused_computation.15 | convolution fusion | flops 21626880 | bytes 6553728 | tf_op jit(solution)/shard_map/cs,sf->cf/dot_general | solution.py:14
  174.3 6.5 %fusion.15 = bf16[4,64,2880]{2,1,0:T(8,128)(2,1)} fusion(bf16[1280,2880]{0,1:T(8,128)(2,1)} %param.11, f32[1,4,64,1280]{3,1,2,0:T(4,128)S(1)} %bitcast.130, f32[4,64]{1,0:T(4,128)S(1)} %add_rsqrt_fusion.1), kind=kOutput, calls=%fused_computation.27 | convolution fusion | flops 1888829440 | bytes 10159104 | tf_op jit(solution)/shard_map/bwd,de->bwe/dot_general | solution.py:14
  180.8 6.3 %reshape.354 = bf16[4,64,3,12,80]{4,3,2,1,0:T(8,128)(2,1)} reshape(bf16[4,64,2880]{2,1,0:T(8,128)(2,1)} %fusion.15) | data formatting | bytes 2949120 | tf_op jit(solution)/shard_map/reshape | solution.py:26
  187.2 3.9 fusion.93
  191.1 4.6 fusion.94
  201.1 3.3 multiply_reduce_fusion.3
  205.6 20.8 %reshape.412 = bf16[32,1,81920]{2,1,0:T(2,128)(2,1)} reshape(bf16[32,2,40960]{2,1,0:T(2,128)(2,1)} %all-to-all-done.2) | data formatting | bytes 10485760
  226.4 9.8 %fusion.6 = f32[4,81920]{1,0:T(4,128)S(1)} fusion(pred[4,32]{1,0:T(4,128)(4,1)S(1)} %get-tuple-element.9, bf16[32,1,81920]{2,1,0:T(2,128)(2,1)} %reshape.412), kind=kOutput, calls=%fused_computation.16 | convolution fusion | flops 21626880 | bytes 6553728 | tf_op jit(solution)/shard_map/cs,sf->cf/dot_general | solution.py:14
  242.8 4.9 fusion.49
  247.6 4.5 fusion.46
  262.4 5.1 convert_element_type.137
  271.2 7.5 %convolution_bitcast_fusion = f32[1280,2880]{1,0:T(8,128)} fusion(bf16[4,64,2880]{2,1,0:T(8,128)(2,1)S(1)} %copy-done.10, bf16[1,4,64,1280]{3,1,2,0:T(4,128)(2,1)S(1)} %bitcast.139), kind=kOutput, calls=%fused_computation.17 | convolution fusion | flops 1887436800 | bytes 16875520 | tf_op jit(solution)/shard_map/bwd,bwe->de/dot_general | solution.py:14
  280.3 3.3 fusion.3
  283.6 7.9 %reduce.8 = bf16[32,81920]{1,0:T(8,128)(2,1)} reduce(bf16[32,1,81920]{2,0,1:T(8,128)(2,1)} %fusion.3, bf16[]{:T(256)} %broadcast.589), dimensions={1}, to_apply=%copy.73.reduce_sub_computation | reduce | bytes 10485762 | tf_op jit(solution)/shard_map/all_to_all | solution.py:150
  291.6 7.7 %reshape.409 = bf16[32,2,40960]{2,1,0:T(2,128)(2,1)} reshape(bf16[32,81920]{1,0:T(8,128)(2,1)} %reduce.8) | data formatting | bytes 10485760
  299.2 6.3 %all-to-all-start.1 = ((bf16[32,2,40960]{2,1,0:T(2,128)(2,1)}), bf16[32,2,40960]{2,1,0:T(2,128)(2,1)}, u32[]{:S(2)}, u32[]{:S(2)}) async-start(bf16[32,2,40960]{2,1,0:T(2,128)(2,1)} %reshape.409), calls=%async_computation.1 | async-start | bytes 10485760 | tf_op jit(solution)/shard_map/all_to_all | solution.py:150
  305.6 129.1 %all-reduce.2 = f32[1280]{0:T(1024)S(1)} all-reduce(f32[1280]{0:T(1024)S(1)} %get-tuple-element.4), channel_id=4, replica_groups=mesh['dp'=32,'vis'=4] {'dp','vis'}, use_global_device_ids=true, to_apply=%region_13.14.clone | all-reduce | flops 1280 | bytes 10240
  435.2 20.7 %reshape.410 = bf16[32,1,81920]{2,1,0:T(2,128)(2,1)} reshape(bf16[32,2,40960]{2,1,0:T(2,128)(2,1)} %all-to-all-done.1) | data formatting | bytes 10485760
  455.9 10.9 %convolution_convert_fusion.3 = bf16[8,81920]{1,0:T(8,128)(2,1)} fusion(bf16[32,1,81920]{2,1,0:T(2,128)(2,1)} %reshape.410, s32[8]{0:T(128)S(1)} %fusion.76, pred[8]{0:T(512)(128)(4,1)S(1)} %compare_bitcast_fusion), kind=kOutput, calls=%fused_computation.12 | convolution fusion | flops 42598912 | bytes 6553640 | tf_op jit(solution)/shard_map/sk,sf->kf/dot_general | solution.py:14
  469.7 85.0 %all-reduce.6.cloned.1.call-done = (f32[1280,2880]{1,0:T(8,128)}, f32[960,1280]{0,1:T(8,128)}) async-done(((f32[1280,2880]{1,0:T(8,128)}, f32[960,1280]{0,1:T(8,128)}), (f32[1280,2880]{1,0:T(8,128)}, f32[960,1280]{0,1:T(8,128)})) %all-reduce.6.cloned.1.call-update) | async-done | bytes 19660816
  (95 shorter events, 50.4 us)
Async XLA Ops:
  7.2 194.0 %copy-start = (bf16[960,1280]{1,0:T(8,128)(2,1)S(1)}, bf16[960,1280]{1,0:T(8,128)(2,1)}, u32[]{:S(2)}) copy-start(bf16[960,1280]{1,0:T(8,128)(2,1)} %param.12) | copy-start | bytes 7372804
  37.6 3.5 copy-start.15
  63.5 71.5 %all-to-all-start = ((bf16[32,2,40960]{2,1,0:T(2,128)(2,1)}), bf16[32,2,40960]{2,1,0:T(2,128)(2,1)}, u32[]{:S(2)}, u32[]{:S(2)}) async-start(bf16[32,2,40960]{2,1,0:T(2,128)(2,1)} %reshape.407), calls=%async_computation | async-start | bytes 10485760 | tf_op jit(solution)/shard_map/all_to_all | solution.py:140
  135.0 70.6 %all-to-all-start.2 = ((bf16[32,2,40960]{2,1,0:T(2,128)(2,1)}), bf16[32,2,40960]{2,1,0:T(2,128)(2,1)}, u32[]{:S(2)}, u32[]{:S(2)}) async-start(bf16[32,2,40960]{2,1,0:T(2,128)(2,1)} %reshape.411), calls=%async_computation.2 | async-start | bytes 10485760 | tf_op jit(solution)/shard_map/all_to_all | solution.py:152
  139.8 414.9 %all-reduce.6.cloned.1.call-start = ((), (), s32[]{:S(2)}) async-start(), calls=%async_computation.3 | async-start | bytes 40632320
  173.3 1.1 copy-start.2
  191.0 4.6 copy-start.5
  226.4 9.8 %copy-start.4 = (f32[4,64,1280]{2,1,0:T(8,128)S(1)}, f32[4,64,1280]{2,1,0:T(8,128)}, u32[]{:S(2)}) copy-start(f32[4,64,1280]{2,1,0:T(8,128)} %get-tuple-element.22) | copy-start | bytes 3932164
  226.4 9.8 %copy-start.14 = (f32[1280]{0:T(1024)S(1)}, f32[1280]{0:T(1024)}, u32[]{:S(2)}) copy-start(f32[1280]{0:T(1024)} %param.13) | copy-start | bytes 15364
  238.1 0.8 copy-start.7
  239.8 1.2 copy-start.6
  241.0 1.7 copy-start.16
  242.8 4.9 copy-start.11
  253.9 1.3 copy-start.8
  255.2 3.2 copy-start.12
  255.2 3.2 copy-start.13
  267.5 2.3 copy-start.3
  269.8 1.4 copy-start.10
  278.7 1.1 copy-start.9
  299.2 136.0 %all-to-all-start.1 = ((bf16[32,2,40960]{2,1,0:T(2,128)(2,1)}), bf16[32,2,40960]{2,1,0:T(2,128)(2,1)}, u32[]{:S(2)}, u32[]{:S(2)}) async-start(bf16[32,2,40960]{2,1,0:T(2,128)(2,1)} %reshape.409), calls=%async_computation.1 | async-start | bytes 10485760 | tf_op jit(solution)/shard_map/all_to_all | solution.py:150
  455.9 102.0 %copy-start.1 = (bf16[960,1280]{1,0:T(8,128)(2,1)S(1)}, bf16[960,1280]{1,0:T(8,128)(2,1)}, u32[]{:S(2)}) copy-start(bf16[960,1280]{1,0:T(8,128)(2,1)} %param.12) | copy-start | bytes 7372804
Sparse Core Ops, SparseCore 0:
  278.8 275.8 all-reduce.5
where the time goes:
time: 575 us; the launch traced here: 565 us
  blocking collectives  151 us (26%)
  local copies, waits for them, and re-layouts  139 us (24%)
  waiting for transfers between devices  128 us (22%)
  matrix products  84.6 us (15%)
  other arithmetic  30.7 us (5%)
  starting transfers between devices  17.1 us (3%)
  between operations  14.8 us (3%)
    unnamed x1, blocking collectives  129 us
    unnamed x47, local copies, waits for them, and re-layouts  97.4 us
    unnamed x2, waiting for transfers between devices  85 us
    dot_general x16, matrix products, contract(): jnp.einsum(formula, first_op, second_op, preferred_element_type=jnp.float32)  80 us
    all_to_all x1, waiting for transfers between devices, on_device(): lax.all_to_all(out_rows, 'dp', split_axis=0, concat_axis=0, tiled=True)  42 us
    all_gather x1, blocking collectives, on_device(): column_live = lax.all_gather(window_live, 'dp', axis=0, tiled=True)  21.8 us
  transfers between devices with their start and end apart: 4, of which 3 were waited for; matrix products, arithmetic and copies ran while one was open for 25% of the time, Pallas kernels for 0%

commit v1 on v0

v1 whole, which is shorter than its diff:
```python
import jax
import jax.numpy as jnp
from jax import lax
from jax.experimental import pallas as pl
from jax.experimental.pallas import tpu as pltpu
from jax.sharding import PartitionSpec as P

D = 1280
HEADS = 12
HD = 80
INNER = HEADS * HD
WIN = 64
SLOTS = 8
ROWS = SLOTS * WIN
PAIRS = SLOTS // 2
EPSILON = 1e-06
NEGATIVE = -1e30
SCALE = HD ** (-0.5)
SHARD = 10
HALF = D // 2
BLOCK = HALF // 4
OUT_AT = 2944
GAIN_AT = OUT_AT + INNER
COLS = 3968
MESH = pl.DeviceIdType.MESH
BF = jnp.bfloat16
F32 = jnp.float32


def mm(a, b):
    return lax.dot_general(a, b, (((1,), (0,)), ((), ())), preferred_element_type=F32)


def mm_nt(a, b):
    return lax.dot_general(a, b, (((1,), (1,)), ((), ())), preferred_element_type=F32)


def mm_tn(a, b):
    return lax.dot_general(a, b, (((0,), (0,)), ((), ())), preferred_element_type=F32)


def stack_pair(compact, left):
    zero = jnp.zeros_like(compact)
    return jnp.concatenate(
        [jnp.where(left, compact, zero), jnp.where(left, zero, compact)], axis=0
    ).astype(BF)


def order_rows(lt_ref, slot, tall):
    for core in range(2):
        for a in range(4):
            for b in range(0, 4, 2):
                pieces = []
                for c in (b, b + 1):
                    y, x = (a, c) if slot == 0 else (c, a)
                    at = ((y * 4 + x) * 2 + core) * 40
                    pieces.append(tall[at:at + 40, :])
                to = a * BLOCK + b * 40
                lt_ref[slot, core, to:to + 80, :] = jnp.concatenate(pieces, axis=0).astype(BF)


def local_kernel(
    live_ref, index_ref, patches_ref, cot_ref, gain_ref, wqkv_hbm, wout_hbm,
    merged_ref, lt_ref, rt_ref, gcol_ref,
    wqkv, wout, tall, tall_z, windows, normed, packed, packed_t, probs, att, d_att, merged_rows, d_ctx_t,
    sems,
):
    cp_qkv = pltpu.make_async_copy(wqkv_hbm, wqkv, sems.at[0])
    cp_out = pltpu.make_async_copy(wout_hbm, wout, sems.at[1])
    cp_qkv.start()
    cp_out.start()
    pick_t = (lax.broadcasted_iota(jnp.int32, (ROWS, ROWS), 0) == index_ref[...]).astype(BF)
    picked = mm_tn(pick_t, patches_ref[...])
    windows[...] = picked.astype(BF)
    inverse = lax.rsqrt(jnp.mean(picked * picked, -1, keepdims=True) + EPSILON)
    normed_rows = (picked * inverse).astype(BF)
    normed[...] = normed_rows
    tall[...] = (picked * inverse).T
    order_rows(lt_ref, 0, tall)
    for core in range(2):
        for z in range(4):
            for x in range(4):
                for y in range(4):
                    to = core * HALF + z * BLOCK + x * 40 + y * SHARD
                    at = ((y * 4 + x) * 2 + core) * 40 + z * SHARD
                    tall_z[to:to + SHARD, :] = tall[at:at + SHARD, :]
    for core in range(2):
        lt_ref[1, core] = tall_z[core * HALF:(core + 1) * HALF, :].astype(BF)
    row_i = lax.broadcasted_iota(jnp.int32, (ROWS, ROWS), 0)
    col_i = lax.broadcasted_iota(jnp.int32, (ROWS, ROWS), 1)
    spread = (row_i == (col_i % 128) * 4 + col_i // 128).astype(BF)
    gather = (col_i == (row_i % 128) * 4 + row_i // 128).astype(BF)
    cp_qkv.wait()
    for start, size in ((0, 640), (640, 640), (1280, 640), (1920, 640), (2560, 320)):
        tile = mm(normed_rows, wqkv[:, start:start + size]).astype(BF)
        packed[:, start:start + size] = tile
        packed_t[start:start + size, :] = tile.T

    lane = lax.broadcasted_iota(jnp.int32, (WIN, 128), 1)
    left = lane < WIN
    key_row = lax.broadcasted_iota(jnp.int32, (WIN, 128), 0)

    def forward(pair, carry):
        cols = pl.ds(pl.multiple_of(pair * 128, 128), 128)
        mask = key_row < jnp.where(left, live_ref[0, 2 * pair], live_ref[0, 2 * pair + 1])
        for h in range(HEADS):
            q_t = packed_t[HD * h:HD * (h + 1), cols]
            v_t = packed_t[2 * INNER + HD * h:2 * INNER + HD * (h + 1), cols]
            k_n = packed[cols, INNER + HD * h:INNER + HD * (h + 1)]
            full = mm(k_n, q_t)
            scores = jnp.where(left, full[:WIN], full[WIN:]) * SCALE
            scores = jnp.where(mask, scores, NEGATIVE)
            top = jnp.max(scores, axis=0, keepdims=True)
            weight = jnp.exp(scores - top)
            prob = weight * (1.0 / jnp.sum(weight, axis=0, keepdims=True))
            probs[pair, h] = prob
            rt_ref[OUT_AT + HD * h:OUT_AT + HD * (h + 1), cols] = mm(
                v_t, stack_pair(prob, left)
            ).astype(BF)
        return carry

    lax.fori_loop(0, PAIRS, forward, 0)
    cp_out.wait()
    ctx = rt_ref[OUT_AT:OUT_AT + INNER, :].T
    cot_rows = jnp.concatenate([cot_ref[:, j * D:(j + 1) * D] for j in range(4)], axis=0)
    for n in range(5):
        cols = slice(256 * n, 256 * (n + 1))
        att[:, cols] = mm(ctx, wout[:, cols]) + windows[:, cols].astype(F32)
        d_att[:, cols] = mm(spread, cot_rows[:, cols]).astype(BF)

    gain = gain_ref[...]

    def norm_block(block, total):
        rows = pl.ds(pl.multiple_of(block * WIN, WIN), WIN)
        alive = (
            lax.broadcasted_iota(jnp.int32, (WIN, 1), 0) < live_ref[0, block]
        ).astype(F32)
        attended = att[rows, :]
        inv = lax.rsqrt(jnp.mean(attended * attended, -1, keepdims=True) + EPSILON)
        normalized = attended * inv
        merged_rows[rows, :] = (normalized * gain * alive).astype(BF)
        grad_rows = d_att[rows, :].astype(F32) * alive
        prod = grad_rows * normalized
        scaled = grad_rows * gain
        mean = jnp.mean(scaled * normalized, -1, keepdims=True)
        d_att[rows, :] = (inv * (scaled - normalized * mean)).astype(BF)
        return total + jnp.sum(prod, axis=0, keepdims=True)

    total = lax.fori_loop(0, SLOTS, norm_block, jnp.zeros((1, D), F32))
    d_rows = d_att[...]
    tall[...] = d_rows.astype(F32).T
    order_rows(lt_ref, 2, tall)
    tall[:, :128] = jnp.broadcast_to(total, (128, D)).T
    for core in range(2):
        for x in range(4):
            for y in range(4):
                at = ((y * 4 + x) * 2 + core) * 40
                to = x * BLOCK + y * 40
                gcol_ref[core, to:to + 40, :] = tall[at:at + 40, :128]
    rt_ref[3 * INNER:OUT_AT, :] = jnp.zeros((OUT_AT - 3 * INNER, ROWS), BF)
    rt_ref[OUT_AT + INNER:, :] = jnp.zeros((COLS - OUT_AT - INNER, ROWS), BF)
    for n in range(5):
        cols = slice(256 * n, 256 * (n + 1))
        back = mm(gather, merged_rows[:, cols]).astype(BF)
        for j in range(4):
            merged_ref[:, j * D + 256 * n:j * D + 256 * (n + 1)] = back[128 * j:128 * (j + 1)]
    for n in range(3):
        d_ctx_t[320 * n:320 * (n + 1), :] = mm_nt(wout[320 * n:320 * (n + 1), :], d_rows).astype(BF)

    def backward(pair, carry):
        cols = pl.ds(pl.multiple_of(pair * 128, 128), 128)
        for h in range(HEADS):
            q_t = packed_t[HD * h:HD * (h + 1), cols]
            k_t = packed_t[INNER + HD * h:INNER + HD * (h + 1), cols]
            v_n = packed[cols, 2 * INNER + HD * h:2 * INNER + HD * (h + 1)]
            dc_t = d_ctx_t[HD * h:HD * (h + 1), cols]
            prob = probs[pair, h]
            full = mm(v_n, dc_t)
            d_prob = jnp.where(left, full[:WIN], full[WIN:])
            total = jnp.sum(d_prob * prob, axis=0, keepdims=True)
            d_score = stack_pair(prob * (d_prob - total) * SCALE, left)
            rt_ref[HD * h:HD * (h + 1), cols] = mm(k_t, d_score).astype(BF)
            rt_ref[INNER + HD * h:INNER + HD * (h + 1), cols] = mm_nt(q_t, d_score).astype(BF)
            rt_ref[2 * INNER + HD * h:2 * INNER + HD * (h + 1), cols] = mm_nt(
                dc_t, stack_pair(prob, left)
            ).astype(BF)
        return carry

    lax.fori_loop(0, PAIRS, backward, 0)


def local_call(patches, window_index, window_live, d_merged, w_qkv, w_out, merge_gain):
    vmem = pl.BlockSpec(memory_space=pltpu.VMEM)
    smem = pl.BlockSpec(memory_space=pltpu.SMEM)
    hbm = pl.BlockSpec(memory_space=pl.ANY)
    return pl.pallas_call(
        local_kernel,
        out_shape=(
            jax.ShapeDtypeStruct((ROWS // 4, 4 * D), BF),
            jax.ShapeDtypeStruct((3, 2, HALF, ROWS), BF),
            jax.ShapeDtypeStruct((COLS, ROWS), BF),
            jax.ShapeDtypeStruct((2, HALF, 128), F32),
        ),
        in_specs=[smem, vmem, vmem, vmem, vmem, hbm, hbm],
        out_specs=(vmem, vmem, vmem, vmem),
        scratch_shapes=[
            pltpu.VMEM((D, 3 * INNER), BF),
            pltpu.VMEM((INNER, D), BF),
            pltpu.VMEM((D, ROWS), F32),
            pltpu.VMEM((D, ROWS), F32),
            pltpu.VMEM((ROWS, D), BF),
            pltpu.VMEM((ROWS, D), BF),
            pltpu.VMEM((ROWS, 3 * INNER), BF),
            pltpu.VMEM((3 * INNER, ROWS), BF),
            pltpu.VMEM((PAIRS, HEADS, WIN, 128), F32),
            pltpu.VMEM((ROWS, D), F32),
            pltpu.VMEM((ROWS, D), BF),
            pltpu.VMEM((ROWS, D), BF),
            pltpu.VMEM((INNER, ROWS), BF),
            pltpu.SemaphoreType.DMA((2,)),
        ],
        compiler_params=pltpu.CompilerParams(vmem_limit_bytes=60 * 2**20),
        cost_estimate=pl.CostEstimate(flops=9_000_000_000, bytes_accessed=20_000_000, transcendentals=400_000),
    )(window_live, window_index, patches, d_merged, merge_gain.reshape(1, D), w_qkv, w_out)


PARTS = (
    (2944, 512, 2, "xyz"),
    (0, 768, 0, "yxz"),
    (1408, 768, 1, "zxy"),
    (3456, 512, 2, "xyz"),
    (768, 640, 0, "yxz"),
    (2176, 768, 1, "zxy"),
)
PER_PART = 13


def sum_kernel(lt_ref, rt_ref, gcol_ref, fq_ref, fo_ref, *scratch):
    sends, recvs = scratch[-2:]
    buffers = [scratch[10 * i:10 * (i + 1)] for i in range(len(PARTS))]
    dp = lax.axis_index("dp")
    core = dp % 2
    place = {"x": (dp // 2) % 4, "y": dp // 8, "z": lax.axis_index("vis")}

    def device(axis=None, step=0):
        at = dict(place)
        if axis is not None:
            at[axis] = (at[axis] + step) % 4
        side = 1 - core if axis is None else core
        return {"dp": (at["y"] * 4 + at["x"]) * 2 + side, "vis": at["z"]}

    partners = [device()] + [device(axis, step) for axis in "xyz" for step in (1, 2, 3)]
    barrier = pltpu.get_barrier_semaphore()
    for partner in partners:
        pl.semaphore_signal(barrier, inc=1, device_id=partner, device_id_type=MESH)

    started = {}

    def send(part, number, src, dst, target):
        copy = pltpu.make_async_remote_copy(
            src_ref=src, dst_ref=dst,
            send_sem=sends.at[PER_PART * part + number],
            recv_sem=recvs.at[PER_PART * part + number],
            device_id=target, device_id_type=MESH,
        )
        copy.start()
        started[part, number] = copy

    def arrived(part, number):
        started[part, number].wait_recv()

    def tiles(part):
        width = PARTS[part][1]
        return [(at, min(256, width - at)) for at in range(0, width, 256)]

    def product(part, side, at, size):
        first, width, slot, route = PARTS[part]
        out = mm_nt(lt_ref[slot, side], rt_ref[first + at:first + at + size, :])
        if first + at + size == COLS:
            gain = gcol_ref[side]
            lane = lax.broadcasted_iota(jnp.int32, gain.shape, 1)
            gain = jnp.where(lane >= GAIN_AT % 128, gain, 0.0)
            out = out + jnp.concatenate([jnp.zeros((HALF, size - 128), F32), gain], axis=1)
        return out

    def make_other(part):
        to_pair = buffers[part][0]
        for at, size in tiles(part):
            to_pair[:, at:at + size] = product(part, 1 - core, at, size).astype(BF)

    def send_other(part):
        send(part, 0, buffers[part][0], buffers[part][1], device())

    def make_own(part):
        route = PARTS[part][3]
        from_pair, own, mid, wide = buffers[part][1:5]
        mine = [product(part, core, at, size) for at, size in tiles(part)]
        arrived(part, 0)
        for (at, size), value in zip(tiles(part), mine):
            value = (value + from_pair[:, at:at + size].astype(F32)).astype(BF)
            for b in range(4):
                own[b, :, at:at + size] = value[BLOCK * b:BLOCK * (b + 1)]
        me = place[route[0]]
        up, down, far = (me + 1) % 4, (me + 3) % 4, (me + 2) % 4
        low, high = pl.ds(0, 80), pl.ds(80, 80)
        send(part, 1, own.at[far, low], mid.at[0], device(route[0], 1))
        send(part, 2, own.at[far, high], mid.at[1], device(route[0], 3))
        send(part, 3, own.at[up, high], wide.at[0, high], device(route[0], 1))
        send(part, 4, own.at[down, low], wide.at[1, low], device(route[0], 3))

    def pass_on(part):
        route = PARTS[part][3]
        own, mid, wide, on = buffers[part][2:6]
        me = place[route[0]]
        up, down = (me + 1) % 4, (me + 3) % 4
        arrived(part, 1)
        on[0] = (own[up, :80, :].astype(F32) + mid[0].astype(F32)).astype(BF)
        send(part, 5, on.at[0], wide.at[0, pl.ds(0, 80)], device(route[0], 1))
        arrived(part, 2)
        on[1] = (own[down, 80:, :].astype(F32) + mid[1].astype(F32)).astype(BF)
        send(part, 6, on.at[1], wide.at[1, pl.ds(80, 80)], device(route[0], 3))

    def second(part):
        route = PARTS[part][3]
        own, mid, wide, on, two, two_in = buffers[part][2:8]
        for number in (3, 4, 5, 6):
            arrived(part, number)
        me = place[route[0]]
        value = own[me].astype(F32) + wide[0].astype(F32) + wide[1].astype(F32)
        value = jnp.concatenate([value, jnp.zeros((8, value.shape[1]), F32)], axis=0)
        for b in range(4):
            two[b] = value[40 * b:40 * b + 48].astype(BF)
        for step in (1, 2, 3):
            to = (place[route[1]] + step) % 4
            send(part, 6 + step, two.at[to], two_in.at[step - 1], device(route[1], step))

    def third(part):
        route = PARTS[part][3]
        two, two_in, three, three_in = buffers[part][6:10]
        value = two[place[route[1]]].astype(F32)
        for step in (1, 2, 3):
            arrived(part, 6 + step)
            value = value + two_in[step - 1].astype(F32)
        for b in range(4):
            three[b] = value[SHARD * b:SHARD * b + 16].astype(BF)
        for step in (1, 2, 3):
            to = (place[route[2]] + step) % 4
            send(part, 9 + step, three.at[to], three_in.at[step - 1], device(route[2], step))

    def finish(part):
        first, width, slot, route = PARTS[part]
        three, three_in = buffers[part][8:10]
        value = three[place[route[2]]].astype(F32)
        for step in (1, 2, 3):
            arrived(part, 9 + step)
            value = value + three_in[step - 1].astype(F32)
        if slot == 2:
            fo_ref[first - OUT_AT:first - OUT_AT + width, :] = value.T
        else:
            fq_ref[:, first:first + width] = value

    make_other(0)
    pl.semaphore_wait(barrier, len(partners))
    send_other(0)
    for part in (1, 2):
        make_other(part)
        send_other(part)
    for part in range(6):
        make_own(part)
        if part < 3:
            make_other(part + 3)
            send_other(part + 3)
    for part in range(6):
        pass_on(part)
    for part in range(6):
        second(part)
    for part in range(6):
        third(part)
    for part in range(6):
        finish(part)
    for copy in started.values():
        copy.wait_send()


def sum_call(lt, rt, gcol):
    vmem = pl.BlockSpec(memory_space=pltpu.VMEM)
    scratch = []
    for first, width, slot, route in PARTS:
        scratch += [
            pltpu.VMEM((HALF, width), BF),
            pltpu.VMEM((HALF, width), BF),
            pltpu.VMEM((4, BLOCK, width), BF),
            pltpu.VMEM((2, 80, width), BF),
            pltpu.VMEM((2, BLOCK, width), BF),
            pltpu.VMEM((2, 80, width), BF),
            pltpu.VMEM((4, 48, width), BF),
            pltpu.VMEM((3, 48, width), BF),
            pltpu.VMEM((4, 16, width), BF),
            pltpu.VMEM((3, 16, width), BF),
        ]
    count = PER_PART * len(PARTS)
    return pl.pallas_call(
        sum_kernel,
        out_shape=(
            jax.ShapeDtypeStruct((16, OUT_AT), F32),
            jax.ShapeDtypeStruct((COLS - OUT_AT, 16), F32),
        ),
        in_specs=[vmem] * 3,
        out_specs=(vmem, vmem),
        scratch_shapes=scratch + [pltpu.SemaphoreType.DMA((count,)), pltpu.SemaphoreType.DMA((count,))],
        compiler_params=pltpu.CompilerParams(
            collective_id=0, has_side_effects=True, vmem_limit_bytes=60 * 2**20
        ),
        cost_estimate=pl.CostEstimate(flops=5_000_000_000, bytes_accessed=10_000_000, transcendentals=0),
    )(lt, rt, gcol)


def on_device(patches, window_index, window_live, d_merged, w_qkv, w_out, merge_gain):
    merged, lt, rt, gcol = local_call(
        patches, window_index, window_live, d_merged, w_qkv, w_out, merge_gain
    )
    fq, fo = sum_call(lt, rt, gcol)
    return merged, fq[:SHARD, :3 * INNER], fo[:INNER, :SHARD], fo[INNER, :SHARD]


def solution(mesh):
    both = ("dp", "vis")
    rows = P(both, None)
    return jax.shard_map(
        on_device,
        mesh=mesh,
        in_specs=(rows, rows, rows, rows, P(), P(), P()),
        out_specs=(rows, rows, P(None, both), P(both)),
        check_vma=False,
    )
```

time: 575 us -> 103 us (0.18); the launches traced: 565 us -> 102 us
  blocking collectives: 151 us -> 0 us
  waiting for transfers between devices: 128 us -> 0 us
  local copies, waits for them, and re-layouts: 139 us -> 16.4 us
  Pallas kernels: 0 us -> 85 us
  matrix products: 84.6 us -> 0 us
  other arithmetic: 30.7 us -> 0 us
  starting transfers between devices: 17.1 us -> 0 us
  between operations: 14.8 us -> 0.65 us
    unnamed x1 -> x0, blocking collectives: 129 us -> none
    unnamed x2 -> x0, waiting for transfers between devices: 85 us -> none
    pallas_call x0 -> x2, Pallas kernels: none -> 85 us  [the longest x1 50.1 us: sum_call(): pl.pallas_call(sum_kernel, out_shape=(jax.ShapeDtypeStruct((16, OUT_AT),...]
    unnamed x47 -> x3, local copies, waits for them, and re-layouts: 97.4 us -> 12.9 us
    dot_general x16 -> x0, matrix products: 80 us -> none  [contract(): jnp.einsum(formula, first_op, second_op, preferred_element_type=jnp.float32)]
    all_to_all x3 -> x0, waiting for transfers between devices: 43.1 us -> none  [the longest x1 42 us: on_device(): lax.all_to_all(out_rows, 'dp', split_axis=0, concat_axis=0, tiled=True)]
    all_to_all x3 -> x0, other arithmetic: 23.9 us -> none  [the longest x1 8.01 us: on_device(): lax.all_to_all(out_rows, 'dp', split_axis=0, concat_axis=0, tiled=True)]
    all_gather x1 -> x0, blocking collectives: 21.8 us -> none  [on_device(): column_live = lax.all_gather(window_live, 'dp', axis=0, tiled=True)]
  transfers between devices with their start and end apart: 4 -> 0, of which waited for: 3 -> 0; matrix products, arithmetic and copies ran while one was open for 25% -> 0% of each run, Pallas kernels for 0% -> 0%
where the time goes in v1:
time: 103 us; the launch traced here: 102 us
  Pallas kernels  85 us (83%)
  local copies, waits for them, and re-layouts  16.4 us (16%)
    pallas_call x1, Pallas kernels, sum_call(): pl.pallas_call(sum_kernel, out_shape=(jax.ShapeDtypeStruct((16, OUT_AT),...  50.1 us
    pallas_call x1, Pallas kernels, local_call(): pl.pallas_call(local_kernel, out_shape=(jax.ShapeDtypeStruct((ROWS // 4,...  34.9 us
    unnamed x3, local copies, waits for them, and re-layouts  12.9 us

profile of v1, /device:TPU:0, one launch (start us, length us, event | category | flops | bytes accessed | tf_op | source)
XLA Modules:
  0.0 102.1 jit_solution(12276202068975049539)
XLA Ops:
  0.6 1.3 %reshape.11.gain_ref = f32[1,1280]{1,0:T(1,128)} reshape(f32[1280]{0:T(1024)} %param.13) | data formatting | bytes 10240 | tf_op jit(solution)/shard_map/reshape | solution.py:224
  1.9 10.4 %copy.11.wqkv_hbm = bf16[1280,2880]{1,0:T(8,128)(2,1)} copy(bf16[1280,2880]{0,1:T(8,128)(2,1)} %param.11) | data formatting | bytes 14745600 | tf_op args[4]
  12.4 34.9 %shard_map.102 = (bf16[128,5120]{1,0:T(8,128)(2,1)}, bf16[3,2,640,512]{3,2,1,0:T(8,128)(2,1)}, bf16[3968,512]{1,0:T(8,128)(2,1)}, f32[2,640,128]{2,1,0:T(8,128)}) custom-call(s32[1,8]{1,0:T(1,128)} %live_ref.1, s32[1,512]{1,0:T(1,128)} %index_ref.1, bf16[512,1280]{1,0:T(8,128)(2,1)} %patches_ref.1, bf16[128,5120]{1,0:T(8,128)(2,1)} %cot_ref.1, ...), custom_call_target="tpu_custom_call" | custom-call | flops 8999999488 | bytes 20000000 | tf_op jit(solution)/shard_map/pallas_call | solution.py:196
  47.3 50.1 %shard_map.103 = (f32[16,2944]{1,0:T(8,128)}, f32[1024,16]{1,0:T(8,128)}) custom-call(bf16[3,2,640,512]{3,2,1,0:T(8,128)(2,1)} %get-tuple-element.11.lt_ref, bf16[3968,512]{1,0:T(8,128)(2,1)} %get-tuple-element.12.rt_ref, f32[2,640,128]{2,1,0:T(8,128)} %get-tuple-element.13.gcol_ref), custom_call_target="tpu_custom_call" | custom-call | flops 5000000000 | bytes 10000000 | tf_op jit(solution)/shard_map/pallas_call | solution.py:402
  97.4 1.2 %slice_bitcast_fusion = f32[10]{0:T(128)} fusion(f32[1024,16]{1,0:T(8,128)} %get-tuple-element.15), kind=kLoop, calls=%fused_computation | loop fusion | bytes 80 | tf_op jit(solution)/shard_map/squeeze | solution.py:423
  98.6 1.1 %slice.10 = f32[960,10]{1,0:T(8,128)S(1)} slice(f32[1024,16]{1,0:T(8,128)} %get-tuple-element.15), slice={[0:960], [0:10]} | slice | bytes 76800 | tf_op jit(solution)/shard_map/slice | solution.py:423
  99.6 0.8 copy.12
  100.4 1.6 %copy.14 = f32[10,2880]{1,0:T(8,128)} copy(f32[10,2880]{1,0:T(8,128)} %bitcast.3) | data formatting | bytes 230400

commit v2 on v1

v2 whole, which is shorter than its diff:
```python
import jax
import jax.numpy as jnp
from jax import lax
from jax.experimental import pallas as pl
from jax.experimental.pallas import tpu as pltpu
from jax.sharding import PartitionSpec as P

D = 1280
HEADS = 12
HD = 80
INNER = HEADS * HD
WIN = 64
SLOTS = 8
ROWS = SLOTS * WIN
PAIRS = SLOTS // 2
EPSILON = 1e-06
NEGATIVE = -1e30
SCALE = HD ** (-0.5)
SHARD = 10
HALF = D // 2
BLOCK = HALF // 4
HEAVY = 8
EARLY_AT = 1024
LATE_AT = EARLY_AT + 3 * HEAVY * HD
LATE_END = LATE_AT + 3 * (HEADS - HEAVY) * HD
COLS = 3968
GAIN_AT = INNER
MESH = pl.DeviceIdType.MESH
BF = jnp.bfloat16
F32 = jnp.float32

ROUTES = ("yxz", "xyz", "zxy")
PARTS = (
    (0, 256, 0),
    (256, 256, 1),
    (512, 512, 2),
    (1024, 768, 0),
    (1792, 512, 1),
    (2304, 640, 2),
    (2944, 256, 0),
    (3200, 256, 1),
    (3456, 512, 2),
)
PER_PART = 13
BUFFERS = 8


def mm(a, b):
    return lax.dot_general(a, b, (((1,), (0,)), ((), ())), preferred_element_type=F32)


def mm_nt(a, b):
    return lax.dot_general(a, b, (((1,), (1,)), ((), ())), preferred_element_type=F32)


def mm_tn(a, b):
    return lax.dot_general(a, b, (((0,), (0,)), ((), ())), preferred_element_type=F32)


def stack_pair(compact, left):
    zero = jnp.zeros_like(compact)
    return jnp.concatenate(
        [jnp.where(left, compact, zero), jnp.where(left, zero, compact)], axis=0
    ).astype(BF)


def folded(width):
    return width % 256 == 0


def second_shape(width):
    return (80, width // 2) if folded(width) else (48, width)


def joined_row(kind, head):
    if head < HEAVY:
        return EARLY_AT + (kind * HEAVY + head) * HD
    return LATE_AT + (kind * (HEADS - HEAVY) + head - HEAVY) * HD


def order_rows(left_ops, operand, tall, tall_z):
    for core in range(2):
        for first in range(4):
            for b in range(0, 4, 2):
                to = first * BLOCK + b * 40
                for route in range(2):
                    pieces = []
                    for c in (b, b + 1):
                        y, x = (first, c) if route == 0 else (c, first)
                        at = ((y * 4 + x) * 2 + core) * 40
                        pieces.append(tall[at:at + 40, :])
                    left_ops[operand, route, core, to:to + 80, :] = jnp.concatenate(
                        pieces, axis=0
                    ).astype(BF)
        for z in range(4):
            for x in range(4):
                for y in range(4):
                    to = core * HALF + z * BLOCK + x * 40 + y * SHARD
                    at = ((y * 4 + x) * 2 + core) * 40 + z * SHARD
                    tall_z[to:to + SHARD, :] = tall[at:at + SHARD, :]
        left_ops[operand, 2, core] = tall_z[core * HALF:(core + 1) * HALF, :].astype(BF)


def main_kernel(
    live_ref, index_ref, gain_ref, patches_hbm, cot_hbm, wqkv_hbm, wout_hbm,
    merged_hbm, final_ref,
    patches, wide_rows, wqkv, wout, tall, tall_z, att, rows_low, packed_t, probs, d_att, d_ctx_t,
    left_ops, right_op, gain_cols, local_sems, *scratch,
):
    sends, recvs = scratch[-2:]
    buffers = [scratch[BUFFERS * i:BUFFERS * (i + 1)] for i in range(len(PARTS))]
    loads = [
        pltpu.make_async_copy(src, dst, local_sems.at[i])
        for i, (src, dst) in enumerate(
            ((patches_hbm, patches), (wqkv_hbm, wqkv), (cot_hbm, wide_rows), (wout_hbm, wout))
        )
    ]
    for load in loads:
        load.start()

    dp = lax.axis_index("dp")
    core = dp % 2
    place = {"x": (dp // 2) % 4, "y": dp // 8, "z": lax.axis_index("vis")}

    def coordinate(at, side):
        return {"dp": (at["y"] * 4 + at["x"]) * 2 + side, "vis": at["z"]}

    pair_device = coordinate(place, 1 - core)
    near = {(axis, step): (place[axis] + step) % 4 for axis in "xyz" for step in (1, 2, 3)}
    devices = {key: coordinate({**place, key[0]: value}, core) for key, value in near.items()}
    barrier = pltpu.get_barrier_semaphore()
    for partner in [pair_device] + list(devices.values()):
        pl.semaphore_signal(barrier, inc=1, device_id=partner, device_id_type=MESH)

    started = {}

    def send(part, number, src, dst, target):
        copy = pltpu.make_async_remote_copy(
            src_ref=src, dst_ref=dst,
            send_sem=sends.at[PER_PART * part + number],
            recv_sem=recvs.at[PER_PART * part + number],
            device_id=target, device_id_type=MESH,
        )
        copy.start()
        started[part, number] = copy

    def arrived(part, number):
        started[part, number].wait_recv()

    def tiles(part):
        width = PARTS[part][1]
        return [(at, min(256, width - at)) for at in range(0, width, 256)]

    def product(part, side, at, size):
        first, width, route = PARTS[part]
        operand = 1 if first < EARLY_AT else 0
        out = mm_nt(left_ops[operand, route, side], right_op[first + at:first + at + size, :])
        if first + at + size == EARLY_AT:
            out = out + jnp.concatenate([jnp.zeros((HALF, size - 128), F32), gain_cols[side]], axis=1)
        return out

    def make_other(part):
        own, from_pair = buffers[part][:2]
        for at, size in tiles(part):
            value = product(part, 1 - core, at, size).astype(BF)
            for b in range(4):
                own[b, :, at:at + size] = value[BLOCK * b:BLOCK * (b + 1)]
        send(part, 0, own, from_pair, pair_device)

    def make_own(part):
        axis = ROUTES[PARTS[part][2]][0]
        own, from_pair, mid, wide = buffers[part][:4]
        started.pop((part, 0)).wait()
        for at, size in tiles(part):
            value = product(part, core, at, size)
            for b in range(4):
                own[b, :, at:at + size] = (
                    value[BLOCK * b:BLOCK * (b + 1)] + from_pair[b, :, at:at + size].astype(F32)
                ).astype(BF)
        up, far, down = (near[axis, step] for step in (1, 2, 3))
        low, high = pl.ds(0, 80), pl.ds(80, 80)
        send(part, 1, own.at[far, low], mid.at[0], devices[axis, 1])
        send(part, 2, own.at[far, high], mid.at[1], devices[axis, 3])
        send(part, 3, own.at[up, high], wide.at[0, high], devices[axis, 1])
        send(part, 4, own.at[down, low], wide.at[1, low], devices[axis, 3])

    def pass_on(part):
        axis = ROUTES[PARTS[part][2]][0]
        own, from_pair, mid, wide = buffers[part][:4]
        up, down = near[axis, 1], near[axis, 3]
        low, high = pl.ds(0, 80), pl.ds(80, 80)
        arrived(part, 1)
        own[up, low, :] = (own[up, low, :].astype(F32) + mid[0].astype(F32)).astype(BF)
        send(part, 5, own.at[up, low], wide.at[0, low], devices[axis, 1])
        arrived(part, 2)
        own[down, high, :] = (own[down, high, :].astype(F32) + mid[1].astype(F32)).astype(BF)
        send(part, 6, own.at[down, high], wide.at[1, high], devices[axis, 3])

    def second(part):
        first, width, route = PARTS[part]
        axis = ROUTES[route][1]
        own, from_pair, mid, wide, two, two_in = buffers[part][:6]
        for number in (3, 4, 5, 6):
            arrived(part, number)
        value = own[place[ROUTES[route][0]]].astype(F32) + wide[0].astype(F32) + wide[1].astype(F32)
        if folded(width):
            for b in range(4):
                rows = value[40 * b:40 * (b + 1)]
                two[b] = jnp.concatenate(
                    [rows[:, :width // 2], rows[:, width // 2:]], axis=0
                ).astype(BF)
        else:
            value = jnp.concatenate([value, jnp.zeros((8, width), F32)], axis=0)
            for b in range(4):
                two[b] = value[40 * b:40 * b + 48].astype(BF)
        for step in (1, 2, 3):
            send(part, 6 + step, two.at[near[axis, step]], two_in.at[step - 1], devices[axis, step])

    def third(part):
        first, width, route = PARTS[part]
        axis = ROUTES[route][2]
        two, two_in, three, three_in = buffers[part][4:8]
        value = two[place[ROUTES[route][1]]].astype(F32)
        for step in (1, 2, 3):
            arrived(part, 6 + step)
            value = value + two_in[step - 1].astype(F32)
        if folded(width):
            value = jnp.concatenate([value[:40], value[40:]], axis=1)
            value = jnp.concatenate([value, jnp.zeros((8, width), F32)], axis=0)
        for b in range(4):
            three[b] = value[SHARD * b:SHARD * b + 16].astype(BF)
        for step in (1, 2, 3):
            send(part, 9 + step, three.at[near[axis, step]], three_in.at[step - 1], devices[axis, step])

    def finish(part):
        first, width, route = PARTS[part]
        three, three_in = buffers[part][6:8]
        value = three[place[ROUTES[route][2]]].astype(F32)
        for step in (1, 2, 3):
            arrived(part, 9 + step)
            value = value + three_in[step - 1].astype(F32)
        final_ref[:, first:first + width] = value

    pick_t = (lax.broadcasted_iota(jnp.int32, (ROWS, ROWS), 0) == index_ref[...]).astype(BF)
    pick = pick_t.T
    loads[0].wait()
    for n in range(5):
        cols = slice(256 * n, 256 * (n + 1))
        att[:, cols] = mm(pick, patches[:, cols])
    for n in range(SLOTS):
        rows = slice(WIN * n, WIN * (n + 1))
        picked = att[rows, :]
        normed = picked * lax.rsqrt(jnp.mean(picked * picked, -1, keepdims=True) + EPSILON)
        rows_low[rows, :] = normed.astype(BF)
    for n in range(5):
        cols = slice(256 * n, 256 * (n + 1))
        tall[cols, :] = rows_low[:, cols].astype(F32).T
    order_rows(left_ops, 0, tall, tall_z)
    right_op[INNER:EARLY_AT, :] = jnp.zeros((EARLY_AT - INNER, ROWS), BF)
    right_op[LATE_END:, :] = jnp.zeros((COLS - LATE_END, ROWS), BF)

    loads[1].wait()
    for n in range(6):
        rows = slice(480 * n, 480 * (n + 1))
        packed_t[rows, :] = mm_nt(wqkv[rows, :], rows_low[...]).astype(BF)

    left = lax.broadcasted_iota(jnp.int32, (WIN, 128), 1) < WIN
    key_row = lax.broadcasted_iota(jnp.int32, (WIN, 128), 0)
    masks = [
        key_row < jnp.where(left, live_ref[0, 2 * pair], live_ref[0, 2 * pair + 1])
        for pair in range(PAIRS)
    ]

    def head_rows(kind, h):
        start = kind * INNER + HD * h
        return slice(start, start + HD) if isinstance(h, int) else pl.ds(pl.multiple_of(start, 16), HD)

    def forward(step, carry):
        todo = [
            (step * 3 + i, pair, slice(128 * pair, 128 * (pair + 1)))
            for i in range(3) for pair in range(PAIRS)
        ]
        fulls = [mm_tn(packed_t[head_rows(1, h), c], packed_t[head_rows(0, h), c]) for h, pair, c in todo]
        stacks = []
        for (h, pair, c), full in zip(todo, fulls):
            scores = jnp.where(left, full[:WIN], full[WIN:]) * SCALE
            scores = jnp.where(masks[pair], scores, NEGATIVE)
            top = jnp.max(scores, axis=0, keepdims=True)
            weight = jnp.exp(scores - top)
            prob = weight * (1.0 / jnp.sum(weight, axis=0, keepdims=True))
            probs[pair, h] = prob
            stacks.append(stack_pair(prob, left))
        for (h, pair, c), stack in zip(todo, stacks):
            right_op[head_rows(0, h), c] = mm(packed_t[head_rows(2, h), c], stack).astype(BF)
        return carry

    lax.fori_loop(0, HEADS // 3, forward, 0)

    row_i = lax.broadcasted_iota(jnp.int32, (ROWS, ROWS), 0)
    col_i = lax.broadcasted_iota(jnp.int32, (ROWS, ROWS), 1)
    spread = (row_i == (col_i % 128) * 4 + col_i // 128).astype(BF)
    gather = (col_i == (row_i % 128) * 4 + row_i // 128).astype(BF)
    loads[2].wait()
    loads[3].wait()
    ctx = right_op[:INNER, :].T
    for n in range(5):
        cols = slice(256 * n, 256 * (n + 1))
        att[:, cols] += mm(ctx, wout[:, cols])
        cot = jnp.concatenate(
            [wide_rows[:, j * D + 256 * n:j * D + 256 * (n + 1)] for j in range(4)], axis=0
        )
        d_att[:, cols] = mm(spread, cot).astype(BF)
    gain = gain_ref[...].reshape(1, D)

    def norm_block(block, total):
        rows = pl.ds(pl.multiple_of(block * WIN, WIN), WIN)
        alive = (
            lax.broadcasted_iota(jnp.int32, (WIN, 1), 0) < live_ref[0, block]
        ).astype(F32)
        attended = att[rows, :]
        inv = lax.rsqrt(jnp.mean(attended * attended, -1, keepdims=True) + EPSILON)
        normalized = attended * inv
        rows_low[rows, :] = (normalized * gain * alive).astype(BF)
        grad_rows = d_att[rows, :].astype(F32) * alive
        prod = grad_rows * normalized
        scaled = grad_rows * gain
        mean = jnp.mean(scaled * normalized, -1, keepdims=True)
        d_att[rows, :] = (inv * (scaled - normalized * mean)).astype(BF)
        return total + jnp.sum(prod, axis=0, keepdims=True)

    total = lax.fori_loop(0, SLOTS, norm_block, jnp.zeros((1, D), F32))
    tall[:, :128] = jnp.broadcast_to(total, (128, D)).T
    lane = lax.broadcasted_iota(jnp.int32, (SHARD, 128), 1)
    for side in range(2):
        for z in range(4):
            for x in range(4):
                for y in range(4):
                    to = z * BLOCK + x * 40 + y * SHARD
                    at = ((y * 4 + x) * 2 + side) * 40 + z * SHARD
                    gain_cols[side, to:to + SHARD, :] = jnp.where(
                        lane >= GAIN_AT % 128, tall[at:at + SHARD, :128], 0.0
                    )
    for n in range(5):
        cols = slice(256 * n, 256 * (n + 1))
        tall[cols, :] = d_att[:, cols].astype(F32).T
    order_rows(left_ops, 1, tall, tall_z)

    pl.semaphore_wait(barrier, 1 + len(devices))
    for part in (0, 1, 2):
        make_other(part)
    for n in range(3):
        rows = slice(320 * n, 320 * (n + 1))
        d_ctx_t[rows, :] = mm_nt(wout[rows, :], d_att[...]).astype(BF)
    for part in (0, 1, 2):
        make_own(part)
    for n in range(5):
        back = mm(gather, rows_low[:, 256 * n:256 * (n + 1)]).astype(BF)
        for j in range(4):
            wide_rows[:, j * D + 256 * n:j * D + 256 * (n + 1)] = back[128 * j:128 * (j + 1)]
    store = pltpu.make_async_copy(wide_rows, merged_hbm, local_sems.at[4])
    store.start()

    def backward(heads):
        todo = [
            (h, pair, slice(128 * pair, 128 * (pair + 1))) for h in heads for pair in range(PAIRS)
        ]
        dcs = [d_ctx_t[head_rows(0, h), c] for h, pair, c in todo]
        fulls = [mm_tn(packed_t[head_rows(2, h), c], dc) for (h, pair, c), dc in zip(todo, dcs)]
        stacks = []
        for (h, pair, c), full in zip(todo, fulls):
            prob = probs[pair, h]
            d_prob = jnp.where(left, full[:WIN], full[WIN:])
            dot = jnp.sum(d_prob * prob, axis=0, keepdims=True)
            stacks.append(stack_pair(prob * (d_prob - dot) * SCALE, left))
        for (h, pair, c), dc in zip(todo, dcs):
            to = joined_row(2, h)
            right_op[to:to + HD, c] = mm_nt(dc, stack_pair(probs[pair, h], left)).astype(BF)
        for (h, pair, c), stack in zip(todo, stacks):
            to = joined_row(0, h)
            right_op[to:to + HD, c] = mm(packed_t[head_rows(1, h), c], stack).astype(BF)
            to = joined_row(1, h)
            right_op[to:to + HD, c] = mm_nt(packed_t[head_rows(0, h), c], stack).astype(BF)

    backward(range(0, 4))
    for part in (0, 1, 2):
        pass_on(part)
    backward(range(4, 8))
    for part in (3, 4, 5):
        make_other(part)
    for part in (0, 1, 2):
        second(part)
    backward(range(8, 12))
    for part in (3, 4, 5):
        make_own(part)
    for part in (6, 7, 8):
        make_other(part)
    for part in (0, 1, 2):
        third(part)
    for part in (6, 7, 8):
        make_own(part)
    for part in (3, 4, 5):
        pass_on(part)
    for part in (0, 1, 2):
        finish(part)
    for part in (6, 7, 8):
        pass_on(part)
    for step in (second, third, finish):
        for part in range(3, 9):
            step(part)
    for copy in started.values():
        copy.wait_send()
    store.wait()


def last_kernel(final_ref, merged_in, merged_ref, qkv_ref, out_ref, gain_ref):
    merged_ref[...] = merged_in[...]
    early, late = HEAVY * HD, (HEADS - HEAVY) * HD
    pieces = []
    for kind in range(3):
        at = EARLY_AT + kind * early
        pieces.append(final_ref[:, at:at + early])
        at = LATE_AT + kind * late
        pieces.append(final_ref[:, at:at + late])
    qkv_ref[...] = jnp.concatenate(pieces, axis=1)[:SHARD]
    out_ref[...] = final_ref[:SHARD, :INNER]
    gain_ref[...] = final_ref[:, EARLY_AT - 128:EARLY_AT].T[GAIN_AT % 128:GAIN_AT % 128 + 1, :SHARD]


def on_device(patches, window_index, window_live, d_merged, w_qkv, w_out, merge_gain):
    vmem = pl.BlockSpec(memory_space=pltpu.VMEM)
    smem = pl.BlockSpec(memory_space=pltpu.SMEM)
    hbm = pl.BlockSpec(memory_space=pl.ANY)
    scratch = [
        pltpu.VMEM((ROWS, D), BF),
        pltpu.VMEM((ROWS // 4, 4 * D), BF),
        pltpu.VMEM((3 * INNER, D), BF),
        pltpu.VMEM((INNER, D), BF),
        pltpu.VMEM((D, ROWS), F32),
        pltpu.VMEM((D, ROWS), F32),
        pltpu.VMEM((ROWS, D), F32),
        pltpu.VMEM((ROWS, D), BF),
        pltpu.VMEM((3 * INNER, ROWS), BF),
        pltpu.VMEM((PAIRS, HEADS, WIN, 128), F32),
        pltpu.VMEM((ROWS, D), BF),
        pltpu.VMEM((INNER, ROWS), BF),
        pltpu.VMEM((2, 3, 2, HALF, ROWS), BF),
        pltpu.VMEM((COLS, ROWS), BF),
        pltpu.VMEM((2, HALF, 128), F32),
        pltpu.SemaphoreType.DMA((5,)),
    ]
    for first, width, route in PARTS:
        shape = second_shape(width)
        scratch += [
            pltpu.VMEM((4, BLOCK, width), BF),
            pltpu.VMEM((4, BLOCK, width), BF),
            pltpu.VMEM((2, 80, width), BF),
            pltpu.VMEM((2, BLOCK, width), BF),
            pltpu.VMEM((4,) + shape, BF),
            pltpu.VMEM((3,) + shape, BF),
            pltpu.VMEM((4, 16, width), BF),
            pltpu.VMEM((3, 16, width), BF),
        ]
    count = PER_PART * len(PARTS)
    scratch += [pltpu.SemaphoreType.DMA((count,)), pltpu.SemaphoreType.DMA((count,))]
    merged, final = pl.pallas_call(
        main_kernel,
        out_shape=(
            jax.ShapeDtypeStruct((ROWS // 4, 4 * D), BF),
            jax.ShapeDtypeStruct((16, COLS), F32),
        ),
        in_specs=[smem, vmem, vmem, hbm, hbm, hbm, hbm],
        out_specs=(hbm, vmem),
        scratch_shapes=scratch,
        compiler_params=pltpu.CompilerParams(
            collective_id=0, has_side_effects=True, vmem_limit_bytes=62 * 2**20
        ),
        cost_estimate=pl.CostEstimate(
            flops=14_000_000_000, bytes_accessed=14_000_000, transcendentals=400_000
        ),
    )(window_live, window_index, merge_gain, patches, d_merged, w_qkv.T, w_out)
    merged, qkv, out, gain = pl.pallas_call(
        last_kernel,
        out_shape=(
            jax.ShapeDtypeStruct((ROWS // 4, 4 * D), BF),
            jax.ShapeDtypeStruct((SHARD, 3 * INNER), F32),
            jax.ShapeDtypeStruct((SHARD, INNER), F32),
            jax.ShapeDtypeStruct((1, SHARD), F32),
        ),
        in_specs=[vmem, vmem],
        out_specs=(vmem, vmem, vmem, vmem),
    )(final, merged)
    return merged, qkv, out.T, gain.reshape(SHARD)


def solution(mesh):
    both = ("dp", "vis")
    rows = P(both, None)
    return jax.shard_map(
        on_device,
        mesh=mesh,
        in_specs=(rows, rows, rows, rows, P(), P(), P()),
        out_specs=(rows, rows, P(None, both), P(both)),
        check_vma=False,
    )
```

time: 103 us -> 70.2 us (0.68)
  local copies, waits for them, and re-layouts: 16.4 us -> 0 us
  Pallas kernels: 85 us -> 69.4 us
    pallas_call x2, Pallas kernels: 85 us -> 69.4 us  [the longest x1 66.7 us: on_device(): pl.pallas_call(main_kernel, out_shape=(jax.ShapeDtypeStruct((ROWS // 4, 4...]
    unnamed x3 -> x0, local copies, waits for them, and re-layouts: 12.9 us -> none
    reshape x1 -> x0, local copies, waits for them, and re-layouts: 1.29 us -> none  [local_call(): merge_gain.reshape(1, D)]
    squeeze x1 -> x0, local copies, waits for them, and re-layouts: 1.19 us -> none  [on_device(): fo[INNER, :SHARD]]
    slice x1 -> x0, local copies, waits for them, and re-layouts: 1.06 us -> none  [on_device(): fo[:INNER, :SHARD]]
where the time goes in v2:
time: 70.2 us; the launch traced here: 70.1 us
  Pallas kernels  69.4 us (99%)
    pallas_call x1, Pallas kernels, on_device(): pl.pallas_call(main_kernel, out_shape=(jax.ShapeDtypeStruct((ROWS // 4, 4...  66.7 us
    pallas_call x1, Pallas kernels, on_device(): pl.pallas_call(last_kernel, out_shape=(jax.ShapeDtypeStruct((ROWS // 4, 4...  2.67 us

profile of v2, /device:TPU:0, one launch (start us, length us, event | category | flops | bytes accessed | tf_op | source)
XLA Modules:
  0.0 70.1 jit_solution(10868810753819458449)
XLA Ops:
  0.6 66.7 %shard_map.102 = (bf16[128,5120]{1,0:T(8,128)(2,1)}, f32[16,3968]{1,0:T(8,128)}) custom-call(s32[1,8]{1,0:T(1,128)} %live_ref.1, s32[1,512]{1,0:T(1,128)} %index_ref.1, f32[1280]{0:T(1024)} %gain_ref.1, bf16[512,1280]{1,0:T(8,128)(2,1)} %patches_hbm.1, bf16[128,5120]{1,0:T(8,128)(2,1)} %cot_hbm.1, bf16[2880,1280]{1,0:T(8,128)(2,1)} %bitcast.3, ...), custom_call_target="tpu_custom_call" | custom-call | flops 14000000000 | bytes 14000000 | tf_op jit(solution)/shard_map/pallas_call | solution.py:465
  67.4 2.7 %shard_map.103 = (bf16[128,5120]{1,0:T(8,128)(2,1)}, f32[10,2880]{1,0:T(8,128)}, f32[10,960]{1,0:T(8,128)}, f32[1,10]{1,0:T(1,128)}) custom-call(f32[16,3968]{1,0:T(8,128)} %get-tuple-element.10.final_ref, bf16[128,5120]{1,0:T(8,128)(2,1)} %get-tuple-element.11.merged_in), custom_call_target="tpu_custom_call" | custom-call | tf_op jit(solution)/shard_map/pallas_call | solution.py:481

commit v3 on v2

--- a/solution.py
+++ b/solution.py
@@ -1,3 +1,5 @@
+import functools
+
 import jax
 import jax.numpy as jnp
 from jax import lax
@@ -19,11 +21,11 @@
 SHARD = 10
 HALF = D // 2
 BLOCK = HALF // 4
-HEAVY = 8
-EARLY_AT = 1024
-LATE_AT = EARLY_AT + 3 * HEAVY * HD
-LATE_END = LATE_AT + 3 * (HEADS - HEAVY) * HD
-COLS = 3968
+GROUPS = ((0, 1024), (1024, 2560), (2560, 3584), (3584, 4096))
+GROUP_HEADS = ((0, 0), (0, 6), (6, 10), (10, 12))
+GROUP_ENDS = tuple(end for _, end in GROUPS)
+COLS = 4096
+OUT_END = GROUPS[0][1]
 GAIN_AT = INNER
 MESH = pl.DeviceIdType.MESH
 BF = jnp.bfloat16
@@ -31,15 +33,10 @@
 
 ROUTES = ("yxz", "xyz", "zxy")
 PARTS = (
-    (0, 256, 0),
-    (256, 256, 1),
-    (512, 512, 2),
-    (1024, 768, 0),
-    (1792, 512, 1),
-    (2304, 640, 2),
-    (2944, 256, 0),
-    (3200, 256, 1),
-    (3456, 512, 2),
+    (0, 256, 0), (256, 256, 1), (512, 512, 2),
+    (1024, 512, 0), (1536, 512, 1), (2048, 512, 2),
+    (2560, 512, 0), (3072, 256, 1), (3328, 256, 2),
+    (3584, 256, 0), (3840, 256, 2),
 )
 PER_PART = 13
 BUFFERS = 8
@@ -73,37 +70,41 @@
 
 
 def joined_row(kind, head):
-    if head < HEAVY:
-        return EARLY_AT + (kind * HEAVY + head) * HD
-    return LATE_AT + (kind * (HEADS - HEAVY) + head - HEAVY) * HD
-
-
-def order_rows(left_ops, operand, tall, tall_z):
-    for core in range(2):
-        for first in range(4):
-            for b in range(0, 4, 2):
-                to = first * BLOCK + b * 40
-                for route in range(2):
-                    pieces = []
-                    for c in (b, b + 1):
-                        y, x = (first, c) if route == 0 else (c, first)
-                        at = ((y * 4 + x) * 2 + core) * 40
-                        pieces.append(tall[at:at + 40, :])
-                    left_ops[operand, route, core, to:to + 80, :] = jnp.concatenate(
-                        pieces, axis=0
-                    ).astype(BF)
-        for z in range(4):
-            for x in range(4):
-                for y in range(4):
-                    to = core * HALF + z * BLOCK + x * 40 + y * SHARD
-                    at = ((y * 4 + x) * 2 + core) * 40 + z * SHARD
-                    tall_z[to:to + SHARD, :] = tall[at:at + SHARD, :]
-        left_ops[operand, 2, core] = tall_z[core * HALF:(core + 1) * HALF, :].astype(BF)
+    for (start, _), (first, end) in zip(GROUPS, GROUP_HEADS):
+        if first <= head < end:
+            return start + (kind * (end - first) + head - first) * HD
+
+
+def order_rows(left_ops, operand, tall, core, first):
+    for b in range(0, 4, 2):
+        to = first * BLOCK + b * 40
+        for route in range(2):
+            pieces = []
+            for c in (b, b + 1):
+                y, x = (first, c) if route == 0 else (c, first)
+                at = ((y * 4 + x) * 2 + core) * 40
+                pieces.append(tall[at:at + 40, :])
+            left_ops[operand, route, core, to:to + 80, :] = jnp.concatenate(
+                pieces, axis=0
+            ).astype(BF)
+
+
+def order_rows_z(left_ops, operand, tall, tall_z, core, z):
+    for x in range(4):
+        for y in range(4):
+            to = core * HALF + z * BLOCK + x * 40 + y * SHARD
+            at = ((y * 4 + x) * 2 + core) * 40 + z * SHARD
+            tall_z[to:to + SHARD, :] = tall[at:at + SHARD, :]
+    to = z * BLOCK
+    left_ops[operand, 2, core, to:to + BLOCK] = tall_z[
+        core * HALF + to:core * HALF + to + BLOCK, :
+    ].astype(BF)
 
 
 def main_kernel(
-    live_ref, index_ref, gain_ref, patches_hbm, cot_hbm, wqkv_hbm, wout_hbm,
-    merged_hbm, final_ref,
+    live_hbm, index_hbm, gain_hbm, patches_hbm, cot_hbm, wqkv_hbm, wout_hbm,
+    merged_hbm, final_hbm,
+    live_ref, index_ref, gain_ref, final_ref,
     patches, wide_rows, wqkv, wout, tall, tall_z, att, rows_low, packed_t, probs, d_att, d_ctx_t,
     left_ops, right_op, gain_cols, local_sems, *scratch,
 ):
@@ -112,7 +113,10 @@
     loads = [
         pltpu.make_async_copy(src, dst, local_sems.at[i])
         for i, (src, dst) in enumerate(
-            ((patches_hbm, patches), (wqkv_hbm, wqkv), (cot_hbm, wide_rows), (wout_hbm, wout))
+            [(index_hbm, index_ref), (patches_hbm, patches), (live_hbm, live_ref), (gain_hbm, gain_ref)]
+            + [(cot_hbm, wide_rows)]
+            + [(wqkv_hbm.at[pl.ds(480 * n, 480)], wqkv.at[pl.ds(480 * n, 480)]) for n in range(6)]
+            + [(wout_hbm, wout)]
         )
     ]
     for load in loads:
@@ -133,6 +137,7 @@
         pl.semaphore_signal(barrier, inc=1, device_id=partner, device_id_type=MESH)
 
     started = {}
+    stored = []
 
     def send(part, number, src, dst, target):
         copy = pltpu.make_async_remote_copy(
@@ -153,9 +158,9 @@
 
     def product(part, side, at, size):
         first, width, route = PARTS[part]
-        operand = 1 if first < EARLY_AT else 0
+        operand = 1 if first < OUT_END else 0
         out = mm_nt(left_ops[operand, route, side], right_op[first + at:first + at + size, :])
-        if first + at + size == EARLY_AT:
+        if first + at + size == OUT_END:
             out = out + jnp.concatenate([jnp.zeros((HALF, size - 128), F32), gain_cols[side]], axis=1)
         return out
 
@@ -240,30 +245,58 @@
             arrived(part, 9 + step)
             value = value + three_in[step - 1].astype(F32)
         final_ref[:, first:first + width] = value
-
+        if first + width in GROUP_ENDS:
+            group = GROUP_ENDS.index(first + width)
+            cols = pl.ds(GROUPS[group][0], first + width - GROUPS[group][0])
+            copy = pltpu.make_async_copy(
+                final_ref.at[:, cols], final_hbm.at[:, cols], local_sems.at[13 + group]
+            )
+            copy.start()
+            stored.append(copy)
+
+    loads[0].wait()
     pick_t = (lax.broadcasted_iota(jnp.int32, (ROWS, ROWS), 0) == index_ref[...]).astype(BF)
     pick = pick_t.T
-    loads[0].wait()
+    loads[1].wait()
     for n in range(5):
         cols = slice(256 * n, 256 * (n + 1))
         att[:, cols] = mm(pick, patches[:, cols])
+    row_i = lax.broadcasted_iota(jnp.int32, (ROWS, ROWS), 0)
+    col_i = lax.broadcasted_iota(jnp.int32, (ROWS, ROWS), 1)
+    spread = (row_i == (col_i % 128) * 4 + col_i // 128).astype(BF)
+    loads[4].wait()
+    for n in range(5):
+        cols = slice(256 * n, 256 * (n + 1))
+        cot = jnp.concatenate(
+            [wide_rows[:, j * D + 256 * n:j * D + 256 * (n + 1)] for j in range(4)], axis=0
+        )
+        d_att[:, cols] = mm(spread, cot).astype(BF)
     for n in range(SLOTS):
         rows = slice(WIN * n, WIN * (n + 1))
         picked = att[rows, :]
         normed = picked * lax.rsqrt(jnp.mean(picked * picked, -1, keepdims=True) + EPSILON)
         rows_low[rows, :] = normed.astype(BF)
-    for n in range(5):
+    for (start, end), (first, last) in zip(GROUPS, GROUP_HEADS):
+        used = start + (3 * HD * (last - first) or INNER)
+        right_op[used:end, :] = jnp.zeros((end - used, ROWS), BF)
+
+    def turn(source, n):
         cols = slice(256 * n, 256 * (n + 1))
-        tall[cols, :] = rows_low[:, cols].astype(F32).T
-    order_rows(left_ops, 0, tall, tall_z)
-    right_op[INNER:EARLY_AT, :] = jnp.zeros((EARLY_AT - INNER, ROWS), BF)
-    right_op[LATE_END:, :] = jnp.zeros((COLS - LATE_END, ROWS), BF)
-
-    loads[1].wait()
+        tall[cols, :] = source[:, cols].astype(F32).T
+
+    corners = [(core, first) for core in range(2) for first in range(4)]
+    beside = [functools.partial(turn, rows_low, n) for n in range(5)]
+    beside += [functools.partial(order_rows, left_ops, 0, tall, *corner) for corner in corners]
+    beside += [functools.partial(order_rows_z, left_ops, 0, tall, tall_z, *corner) for corner in corners]
     for n in range(6):
         rows = slice(480 * n, 480 * (n + 1))
+        loads[5 + n].wait()
         packed_t[rows, :] = mm_nt(wqkv[rows, :], rows_low[...]).astype(BF)
-
+        for piece in beside[4 * n:4 * n + 4]:
+            piece()
+
+    loads[2].wait()
+    loads[3].wait()
     left = lax.broadcasted_iota(jnp.int32, (WIN, 128), 1) < WIN
     key_row = lax.broadcasted_iota(jnp.int32, (WIN, 128), 0)
     masks = [
@@ -296,20 +329,11 @@
 
     lax.fori_loop(0, HEADS // 3, forward, 0)
 
-    row_i = lax.broadcasted_iota(jnp.int32, (ROWS, ROWS), 0)
-    col_i = lax.broadcasted_iota(jnp.int32, (ROWS, ROWS), 1)
-    spread = (row_i == (col_i % 128) * 4 + col_i // 128).astype(BF)
-    gather = (col_i == (row_i % 128) * 4 + row_i // 128).astype(BF)
-    loads[2].wait()
-    loads[3].wait()
+    loads[11].wait()
     ctx = right_op[:INNER, :].T
     for n in range(5):
         cols = slice(256 * n, 256 * (n + 1))
         att[:, cols] += mm(ctx, wout[:, cols])
-        cot = jnp.concatenate(
-            [wide_rows[:, j * D + 256 * n:j * D + 256 * (n + 1)] for j in range(4)], axis=0
-        )
-        d_att[:, cols] = mm(spread, cot).astype(BF)
     gain = gain_ref[...].reshape(1, D)
 
     def norm_block(block, total):
@@ -320,7 +344,7 @@
         attended = att[rows, :]
         inv = lax.rsqrt(jnp.mean(attended * attended, -1, keepdims=True) + EPSILON)
         normalized = attended * inv
-        rows_low[rows, :] = (normalized * gain * alive).astype(BF)
+        patches[rows, :] = (normalized * gain * alive).astype(BF)
         grad_rows = d_att[rows, :].astype(F32) * alive
         prod = grad_rows * normalized
         scaled = grad_rows * gain
@@ -329,6 +353,15 @@
         return total + jnp.sum(prod, axis=0, keepdims=True)
 
     total = lax.fori_loop(0, SLOTS, norm_block, jnp.zeros((1, D), F32))
+    for n in range(5):
+        turn(d_att, n)
+    for corner in corners:
+        order_rows(left_ops, 1, tall, *corner)
+    pl.semaphore_wait(barrier, 1 + len(devices))
+    make_other(0)
+    make_other(1)
+    for corner in corners:
+        order_rows_z(left_ops, 1, tall, tall_z, *corner)
     tall[:, :128] = jnp.broadcast_to(total, (128, D)).T
     lane = lax.broadcasted_iota(jnp.int32, (SHARD, 128), 1)
     for side in range(2):
@@ -340,26 +373,10 @@
                     gain_cols[side, to:to + SHARD, :] = jnp.where(
                         lane >= GAIN_AT % 128, tall[at:at + SHARD, :128], 0.0
                     )
-    for n in range(5):
-        cols = slice(256 * n, 256 * (n + 1))
-        tall[cols, :] = d_att[:, cols].astype(F32).T
-    order_rows(left_ops, 1, tall, tall_z)
-
-    pl.semaphore_wait(barrier, 1 + len(devices))
-    for part in (0, 1, 2):
-        make_other(part)
+    make_other(2)
     for n in range(3):
         rows = slice(320 * n, 320 * (n + 1))
         d_ctx_t[rows, :] = mm_nt(wout[rows, :], d_att[...]).astype(BF)
-    for part in (0, 1, 2):
-        make_own(part)
-    for n in range(5):
-        back = mm(gather, rows_low[:, 256 * n:256 * (n + 1)]).astype(BF)
-        for j in range(4):
-            wide_rows[:, j * D + 256 * n:j * D + 256 * (n + 1)] = back[128 * j:128 * (j + 1)]
-    store = pltpu.make_async_copy(wide_rows, merged_hbm, local_sems.at[4])
-    store.start()
-
     def backward(heads):
         todo = [
             (h, pair, slice(128 * pair, 128 * (pair + 1))) for h in heads for pair in range(PAIRS)
@@ -381,56 +398,67 @@
             to = joined_row(1, h)
             right_op[to:to + HD, c] = mm_nt(packed_t[head_rows(0, h), c], stack).astype(BF)
 
-    backward(range(0, 4))
-    for part in (0, 1, 2):
-        pass_on(part)
-    backward(range(4, 8))
-    for part in (3, 4, 5):
-        make_other(part)
-    for part in (0, 1, 2):
-        second(part)
-    backward(range(8, 12))
-    for part in (3, 4, 5):
-        make_own(part)
-    for part in (6, 7, 8):
-        make_other(part)
-    for part in (0, 1, 2):
-        third(part)
-    for part in (6, 7, 8):
-        make_own(part)
-    for part in (3, 4, 5):
-        pass_on(part)
-    for part in (0, 1, 2):
-        finish(part)
-    for part in (6, 7, 8):
-        pass_on(part)
-    for step in (second, third, finish):
-        for part in range(3, 9):
-            step(part)
+    def each(step, group):
+        start, end = GROUPS[group]
+        for part, (first, width, route) in enumerate(PARTS):
+            if start <= first < end:
+                step(part)
+
+    each(make_own, 0)
+    backward(range(0, 6))
+    each(make_other, 1)
+    backward(range(6, 10))
+    each(make_own, 1)
+    each(make_other, 2)
+    backward(range(10, 12))
+    each(pass_on, 0)
+    each(make_own, 2)
+    each(make_other, 3)
+    gather = (col_i == (row_i % 128) * 4 + row_i // 128).astype(BF)
+    for n in range(5):
+        back = mm(gather, patches[:, 256 * n:256 * (n + 1)]).astype(BF)
+        for j in range(4):
+            wide_rows[:, j * D + 256 * n:j * D + 256 * (n + 1)] = back[128 * j:128 * (j + 1)]
+    store = pltpu.make_async_copy(wide_rows, merged_hbm, local_sems.at[12])
+    store.start()
+
+    each(make_own, 3)
+    each(second, 0)
+    for group in (1, 2, 3):
+        each(pass_on, group)
+    each(third, 0)
+    for group in (1, 2, 3):
+        each(second, group)
+    each(finish, 0)
+    for step in (third, finish):
+        for group in (1, 2, 3):
+            each(step, group)
     for copy in started.values():
         copy.wait_send()
-    store.wait()
+    for copy in stored + [store]:
+        copy.wait()
 
 
 def last_kernel(final_ref, merged_in, merged_ref, qkv_ref, out_ref, gain_ref):
     merged_ref[...] = merged_in[...]
-    early, late = HEAVY * HD, (HEADS - HEAVY) * HD
     pieces = []
     for kind in range(3):
-        at = EARLY_AT + kind * early
-        pieces.append(final_ref[:, at:at + early])
-        at = LATE_AT + kind * late
-        pieces.append(final_ref[:, at:at + late])
+        for (start, _), (first, end) in zip(GROUPS[1:], GROUP_HEADS[1:]):
+            width = HD * (end - first)
+            pieces.append(final_ref[:, start + kind * width:start + (kind + 1) * width])
     qkv_ref[...] = jnp.concatenate(pieces, axis=1)[:SHARD]
     out_ref[...] = final_ref[:SHARD, :INNER]
-    gain_ref[...] = final_ref[:, EARLY_AT - 128:EARLY_AT].T[GAIN_AT % 128:GAIN_AT % 128 + 1, :SHARD]
+    gain_ref[...] = final_ref[:, OUT_END - 128:OUT_END].T[GAIN_AT % 128:GAIN_AT % 128 + 1, :SHARD]
 
 
 def on_device(patches, window_index, window_live, d_merged, w_qkv, w_out, merge_gain):
     vmem = pl.BlockSpec(memory_space=pltpu.VMEM)
-    smem = pl.BlockSpec(memory_space=pltpu.SMEM)
     hbm = pl.BlockSpec(memory_space=pl.ANY)
     scratch = [
+        pltpu.SMEM((1, SLOTS), jnp.int32),
+        pltpu.VMEM((1, ROWS), jnp.int32),
+        pltpu.VMEM((D,), F32),
+        pltpu.VMEM((16, COLS), F32),
         pltpu.VMEM((ROWS, D), BF),
         pltpu.VMEM((ROWS // 4, 4 * D), BF),
         pltpu.VMEM((3 * INNER, D), BF),
@@ -446,7 +474,7 @@
         pltpu.VMEM((2, 3, 2, HALF, ROWS), BF),
         pltpu.VMEM((COLS, ROWS), BF),
         pltpu.VMEM((2, HALF, 128), F32),
-        pltpu.SemaphoreType.DMA((5,)),
+        pltpu.SemaphoreType.DMA((17,)),
     ]
     for first, width, route in PARTS:
         shape = second_shape(width)
@@ -468,8 +496,8 @@
             jax.ShapeDtypeStruct((ROWS // 4, 4 * D), BF),
             jax.ShapeDtypeStruct((16, COLS), F32),
         ),
-        in_specs=[smem, vmem, vmem, hbm, hbm, hbm, hbm],
-        out_specs=(hbm, vmem),
+        in_specs=[hbm] * 7,
+        out_specs=(hbm, hbm),
         scratch_shapes=scratch,
         compiler_params=pltpu.CompilerParams(
             collective_id=0, has_side_effects=True, vmem_limit_bytes=62 * 2**20

time: 70.2 us -> 66.6 us (0.949)
  Pallas kernels: 69.4 us -> 65.8 us
    pallas_call x1, Pallas kernels: 66.7 us -> 63.2 us  [on_device(): pl.pallas_call(main_kernel, out_shape=(jax.ShapeDtypeStruct((ROWS // 4, 4...]
where the time goes in v3:
time: 66.6 us; the launch traced here: 66.5 us
  Pallas kernels  65.8 us (99%)
    pallas_call x1, Pallas kernels, on_device(): pl.pallas_call(main_kernel, out_shape=(jax.ShapeDtypeStruct((ROWS // 4, 4...  63.2 us
    pallas_call x1, Pallas kernels, on_device(): pl.pallas_call(last_kernel, out_shape=(jax.ShapeDtypeStruct((ROWS // 4, 4...  2.65 us

profile of v3, /device:TPU:0, one launch (start us, length us, event | category | flops | bytes accessed | tf_op | source)
XLA Modules:
  0.0 66.5 jit_solution(9687714870087047820)
XLA Ops:
  0.6 63.2 %shard_map.102 = (bf16[128,5120]{1,0:T(8,128)(2,1)}, f32[16,4096]{1,0:T(8,128)}) custom-call(s32[1,8]{1,0:T(1,128)} %live_hbm.1, s32[1,512]{1,0:T(1,128)} %index_hbm.1, f32[1280]{0:T(1024)} %gain_hbm.1, bf16[512,1280]{1,0:T(8,128)(2,1)} %patches_hbm.1, bf16[128,5120]{1,0:T(8,128)(2,1)} %cot_hbm.1, bf16[2880,1280]{1,0:T(8,128)(2,1)} %bitcast.3, ...), custom_call_target="tpu_custom_call" | custom-call | flops 14000000000 | bytes 14000000 | tf_op jit(solution)/shard_map/pallas_call | solution.py:493
  63.8 2.7 %shard_map.103 = (bf16[128,5120]{1,0:T(8,128)(2,1)}, f32[10,2880]{1,0:T(8,128)}, f32[10,960]{1,0:T(8,128)}, f32[1,10]{1,0:T(1,128)}) custom-call(f32[16,4096]{1,0:T(8,128)} %get-tuple-element.10.final_ref, bf16[128,5120]{1,0:T(8,128)(2,1)} %get-tuple-element.11.merged_in), custom_call_target="tpu_custom_call" | custom-call | tf_op jit(solution)/shard_map/pallas_call | solution.py:509

commit v4 on v3

--- a/solution.py
+++ b/solution.py
@@ -31,11 +31,11 @@
 BF = jnp.bfloat16
 F32 = jnp.float32
 
-ROUTES = ("yxz", "xyz", "zxy")
+ROUTES = ("yxz", "xzy", "zyx")
 PARTS = (
     (0, 256, 0), (256, 256, 1), (512, 512, 2),
     (1024, 512, 0), (1536, 512, 1), (2048, 512, 2),
-    (2560, 512, 0), (3072, 256, 1), (3328, 256, 2),
+    (2560, 256, 0), (2816, 512, 1), (3328, 256, 2),
     (3584, 256, 0), (3840, 256, 2),
 )
 PER_PART = 13
@@ -75,29 +75,30 @@
             return start + (kind * (end - first) + head - first) * HD
 
 
+def fine_row(route, first, second, third, core):
+    at = dict(zip(ROUTES[route], (first, second, third)))
+    return ((at["y"] * 4 + at["x"]) * 2 + core) * 40 + at["z"] * SHARD
+
+
 def order_rows(left_ops, operand, tall, core, first):
     for b in range(0, 4, 2):
         to = first * BLOCK + b * 40
-        for route in range(2):
-            pieces = []
-            for c in (b, b + 1):
-                y, x = (first, c) if route == 0 else (c, first)
-                at = ((y * 4 + x) * 2 + core) * 40
-                pieces.append(tall[at:at + 40, :])
-            left_ops[operand, route, core, to:to + 80, :] = jnp.concatenate(
-                pieces, axis=0
-            ).astype(BF)
-
-
-def order_rows_z(left_ops, operand, tall, tall_z, core, z):
-    for x in range(4):
-        for y in range(4):
-            to = core * HALF + z * BLOCK + x * 40 + y * SHARD
-            at = ((y * 4 + x) * 2 + core) * 40 + z * SHARD
+        pieces = []
+        for c in (b, b + 1):
+            at = fine_row(0, first, c, 0, core)
+            pieces.append(tall[at:at + 40, :])
+        left_ops[operand, 0, core, to:to + 80, :] = jnp.concatenate(pieces, axis=0).astype(BF)
+
+
+def order_rows_fine(left_ops, operand, tall, tall_z, route, core, first):
+    base = core * HALF + first * BLOCK
+    for second in range(4):
+        for third in range(4):
+            to = base + second * 40 + third * SHARD
+            at = fine_row(route, first, second, third, core)
             tall_z[to:to + SHARD, :] = tall[at:at + SHARD, :]
-    to = z * BLOCK
-    left_ops[operand, 2, core, to:to + BLOCK] = tall_z[
-        core * HALF + to:core * HALF + to + BLOCK, :
+    left_ops[operand, route, core, first * BLOCK:(first + 1) * BLOCK] = tall_z[
+        base:base + BLOCK, :
     ].astype(BF)
 
 
@@ -287,12 +288,16 @@
     corners = [(core, first) for core in range(2) for first in range(4)]
     beside = [functools.partial(turn, rows_low, n) for n in range(5)]
     beside += [functools.partial(order_rows, left_ops, 0, tall, *corner) for corner in corners]
-    beside += [functools.partial(order_rows_z, left_ops, 0, tall, tall_z, *corner) for corner in corners]
+    for route in (1, 2):
+        beside += [
+            functools.partial(order_rows_fine, left_ops, 0, tall, tall_z, route, *corner)
+            for corner in corners
+        ]
     for n in range(6):
         rows = slice(480 * n, 480 * (n + 1))
         loads[5 + n].wait()
         packed_t[rows, :] = mm_nt(wqkv[rows, :], rows_low[...]).astype(BF)
-        for piece in beside[4 * n:4 * n + 4]:
+        for piece in beside[5 * n:5 * n + 5]:
             piece()
 
     loads[2].wait()
@@ -359,17 +364,19 @@
         order_rows(left_ops, 1, tall, *corner)
     pl.semaphore_wait(barrier, 1 + len(devices))
     make_other(0)
+    for corner in corners:
+        order_rows_fine(left_ops, 1, tall, tall_z, 1, *corner)
     make_other(1)
     for corner in corners:
-        order_rows_z(left_ops, 1, tall, tall_z, *corner)
+        order_rows_fine(left_ops, 1, tall, tall_z, 2, *corner)
     tall[:, :128] = jnp.broadcast_to(total, (128, D)).T
     lane = lax.broadcasted_iota(jnp.int32, (SHARD, 128), 1)
     for side in range(2):
-        for z in range(4):
-            for x in range(4):
-                for y in range(4):
-                    to = z * BLOCK + x * 40 + y * SHARD
-                    at = ((y * 4 + x) * 2 + side) * 40 + z * SHARD
+        for first in range(4):
+            for second_place in range(4):
+                for third_place in range(4):
+                    to = first * BLOCK + second_place * 40 + third_place * SHARD
+                    at = fine_row(2, first, second_place, third_place, side)
                     gain_cols[side, to:to + SHARD, :] = jnp.where(
                         lane >= GAIN_AT % 128, tall[at:at + SHARD, :128], 0.0
                     )

time: 66.6 us -> 64.8 us (0.973)
  Pallas kernels: 65.8 us -> 64 us
    pallas_call x1, Pallas kernels: 63.2 us -> 61.4 us  [on_device(): pl.pallas_call(main_kernel, out_shape=(jax.ShapeDtypeStruct((ROWS // 4, 4...]
where the time goes in v4:
time: 64.8 us; the launch traced here: 64.7 us
  Pallas kernels  64 us (99%)
    pallas_call x1, Pallas kernels, on_device(): pl.pallas_call(main_kernel, out_shape=(jax.ShapeDtypeStruct((ROWS // 4, 4...  61.4 us
    pallas_call x1, Pallas kernels, on_device(): pl.pallas_call(last_kernel, out_shape=(jax.ShapeDtypeStruct((ROWS // 4, 4...  2.65 us

profile of v4, /device:TPU:0, one launch (start us, length us, event | category | flops | bytes accessed | tf_op | source)
XLA Modules:
  0.0 64.7 jit_solution(14729992046650254044)
XLA Ops:
  0.6 61.4 %shard_map.102 = (bf16[128,5120]{1,0:T(8,128)(2,1)}, f32[16,4096]{1,0:T(8,128)}) custom-call(s32[1,8]{1,0:T(1,128)} %live_hbm.1, s32[1,512]{1,0:T(1,128)} %index_hbm.1, f32[1280]{0:T(1024)} %gain_hbm.1, bf16[512,1280]{1,0:T(8,128)(2,1)} %patches_hbm.1, bf16[128,5120]{1,0:T(8,128)(2,1)} %cot_hbm.1, bf16[2880,1280]{1,0:T(8,128)(2,1)} %bitcast.3, ...), custom_call_target="tpu_custom_call" | custom-call | flops 14000000000 | bytes 14000000 | tf_op jit(solution)/shard_map/pallas_call | solution.py:500
  62.0 2.7 %shard_map.103 = (bf16[128,5120]{1,0:T(8,128)(2,1)}, f32[10,2880]{1,0:T(8,128)}, f32[10,960]{1,0:T(8,128)}, f32[1,10]{1,0:T(1,128)}) custom-call(f32[16,4096]{1,0:T(8,128)} %get-tuple-element.10.final_ref, bf16[128,5120]{1,0:T(8,128)(2,1)} %get-tuple-element.11.merged_in), custom_call_target="tpu_custom_call" | custom-call | tf_op jit(solution)/shard_map/pallas_call | solution.py:516

commit v5 on v4

--- a/solution.py
+++ b/solution.py
@@ -421,6 +421,7 @@
     each(pass_on, 0)
     each(make_own, 2)
     each(make_other, 3)
+    each(make_own, 3)
     gather = (col_i == (row_i % 128) * 4 + row_i // 128).astype(BF)
     for n in range(5):
         back = mm(gather, patches[:, 256 * n:256 * (n + 1)]).astype(BF)
@@ -429,7 +430,6 @@
     store = pltpu.make_async_copy(wide_rows, merged_hbm, local_sems.at[12])
     store.start()
 
-    each(make_own, 3)
     each(second, 0)
     for group in (1, 2, 3):
         each(pass_on, group)

time: 64.8 us -> 64.5 us (level)
  no operation moved by 1% of the time
where the time goes in v5:
time: 64.5 us; the launch traced here: 64.3 us
  Pallas kernels  63.7 us (99%)
    pallas_call x1, Pallas kernels, on_device(): pl.pallas_call(main_kernel, out_shape=(jax.ShapeDtypeStruct((ROWS // 4, 4...  61 us
    pallas_call x1, Pallas kernels, on_device(): pl.pallas_call(last_kernel, out_shape=(jax.ShapeDtypeStruct((ROWS // 4, 4...  2.65 us

profile of v5, /device:TPU:0, one launch (start us, length us, event | category | flops | bytes accessed | tf_op | source)
XLA Modules:
  0.0 64.3 jit_solution(9905741484090215288)
XLA Ops:
  0.6 61.0 %shard_map.102 = (bf16[128,5120]{1,0:T(8,128)(2,1)}, f32[16,4096]{1,0:T(8,128)}) custom-call(s32[1,8]{1,0:T(1,128)} %live_hbm.1, s32[1,512]{1,0:T(1,128)} %index_hbm.1, f32[1280]{0:T(1024)} %gain_hbm.1, bf16[512,1280]{1,0:T(8,128)(2,1)} %patches_hbm.1, bf16[128,5120]{1,0:T(8,128)(2,1)} %cot_hbm.1, bf16[2880,1280]{1,0:T(8,128)(2,1)} %bitcast.3, ...), custom_call_target="tpu_custom_call" | custom-call | flops 14000000000 | bytes 14000000 | tf_op jit(solution)/shard_map/pallas_call | solution.py:500
  61.7 2.7 %shard_map.103 = (bf16[128,5120]{1,0:T(8,128)(2,1)}, f32[10,2880]{1,0:T(8,128)}, f32[10,960]{1,0:T(8,128)}, f32[1,10]{1,0:T(1,128)}) custom-call(f32[16,4096]{1,0:T(8,128)} %get-tuple-element.10.final_ref, bf16[128,5120]{1,0:T(8,128)(2,1)} %get-tuple-element.11.merged_in), custom_call_target="tpu_custom_call" | custom-call | tf_op jit(solution)/shard_map/pallas_call | solution.py:516
